TPU v7x, 128 devices: a whole 4x4x4 slice. The times are simulated.
128 devices in a mesh: fsdp: 8 (over z, x_lo), cp: 8 (over y, x_hi), tp: 2 (over core).
Axes of the slice: x: 4 (x_hi: 2, x_lo: 2; x = x_hi * 2 + x_lo), y: 4, z: 4, core: 2. Of those that a mesh axis runs over, the one named last changes fastest.
Arguments:
- tokens: bfloat16 [16, 1024, 2048], P('fsdp', 'cp'), may hold values from -6 to 6
- segment_ids: int32 [16, 1024], P('fsdp', 'cp'), may hold values from 0 to 3, as said below
- cotangent: bfloat16 [16, 1024, 2048], P('fsdp', 'cp'), may hold values from -6 to 6
- norm1_gain: bfloat16 [2048], P(('fsdp', 'cp')), may hold values from 0.5 to 1.5
- q_weight: bfloat16 [2048, 2048], P(('fsdp', 'cp'), 'tp'), may hold values from -0.125 to 0.125
- k_weight: bfloat16 [2048, 256], P(('fsdp', 'cp'), 'tp'), may hold values from -0.125 to 0.125
- v_weight: bfloat16 [2048, 256], P(('fsdp', 'cp'), 'tp'), may hold values from -0.125 to 0.125
- o_weight: bfloat16 [2048, 2048], P(('fsdp', 'cp'), 'tp'), may hold values from -0.5 to 0.5
- norm2_gain: bfloat16 [2048], P(('fsdp', 'cp')), may hold values from 0.5 to 1.5
- gate_weight: bfloat16 [2048, 5632], P(('fsdp', 'cp'), 'tp'), may hold values from -0.125 to 0.125
- up_weight: bfloat16 [2048, 5632], P(('fsdp', 'cp'), 'tp'), may hold values from -0.125 to 0.125
- down_weight: bfloat16 [2048, 5632], P(('fsdp', 'cp'), 'tp'), may hold values from -0.078125 to 0.078125
Outputs:
- out: bfloat16 [16, 1024, 2048], P('fsdp', 'cp')
- x_grad: bfloat16 [16, 1024, 2048], P('fsdp', 'cp')
- norm1_gain_grad: float32 [2048], P(('fsdp', 'cp'))
- q_weight_grad: float32 [2048, 2048], P(('fsdp', 'cp'), 'tp')
- k_weight_grad: float32 [2048, 256], P(('fsdp', 'cp'), 'tp')
- v_weight_grad: float32 [2048, 256], P(('fsdp', 'cp'), 'tp')
- o_weight_grad: float32 [2048, 2048], P(('fsdp', 'cp'), 'tp')
- norm2_gain_grad: float32 [2048], P(('fsdp', 'cp'))
- gate_weight_grad: float32 [2048, 5632], P(('fsdp', 'cp'), 'tp')
- up_weight_grad: float32 [2048, 5632], P(('fsdp', 'cp'), 'tp')
- down_weight_grad: float32 [2048, 5632], P(('fsdp', 'cp'), 'tp')
Inputs may be any that keep to these rules, and one draw needn't show every extreme that they name: `segment_ids`: taken in the order of true positions pos, each sequence's segment numbers never fall.
All inputs are finite; a program needn't handle non-finite values.
Results may differ from a plain program's by a relative error of at most 0.018.
Values may be sent and summed in bfloat16 or wider, within the bound.
No kernel may reach another device: no remote copies, remote signals or barrier semaphores. Data moves between devices by JAX's collectives and lax.ppermute only.
A program may use at most 384 MiB of HBM per device.

v0:
```python
import math

import jax
import jax.numpy as jnp
from jax import lax
from jax.sharding import PartitionSpec as P

HEAD_DIM = 64


NORM_EPS = 1e-05
ROPE_BASE = 10000.0


def copy_for_each(x, axis):
    copies = jnp.broadcast_to(x, (lax.axis_size(axis), *x.shape))
    return lax.all_to_all(copies, axis, split_axis=0, concat_axis=0, tiled=True)


def laid_out(tiles, dim):
    tiles = jnp.moveaxis(tiles, 0, dim)
    shape = tiles.shape
    return tiles.reshape(*shape[:dim], shape[dim] * shape[dim + 1], *shape[dim + 2 :])


def gather_directly(x, axis, dim):
    tiles = copy_for_each(x, axis)
    return laid_out(tiles, dim)


def sent_together(arrays, axis, dim, along):
    widths = [math.prod(a.shape[along:]) for a in arrays]
    both = jnp.concatenate(
        [a.reshape(*a.shape[:along], w) for a, w in zip(arrays, widths)], axis=along
    )
    result = lax.all_gather(both, axis, axis=dim, tiled=True)
    tiles = jnp.split(result, [sum(widths[:k]) for k in range(1, len(widths))], axis=along)
    return tuple(
        (b.reshape(*result.shape[:along], *a.shape[along:]) for a, b in zip(arrays, tiles))
    )


def side_by_side(arrays, axis, dim, along):
    both = jnp.concatenate(arrays, axis=along)
    result, at, outs = (lax.all_gather(both, axis, axis=dim, tiled=True), 0, [])
    for a in arrays:
        outs.append(lax.slice_in_dim(result, at, at + a.shape[along], axis=along))
        at += a.shape[along]
    return tuple(outs)


def over_copies(x, axis):
    everything = copy_for_each(x, axis)
    return jnp.sum(everything, axis=0)


def taken_together(x, axis):
    return copy_for_each(x, axis).astype(jnp.float32).sum(axis=0)


def in_one_piece(arrays, axis, dim, along):
    widths = [a.shape[along] for a in arrays]
    both = jnp.concatenate(arrays, axis=along)
    result = lax.psum_scatter(both, axis, scatter_dimension=dim, tiled=True)
    return tuple(jnp.split(result, [sum(widths[:k]) for k in range(1, len(widths))], axis=along))


def side_by_side_2(arrays, axis, dim, along):
    columns = [a.reshape(*a.shape[:along], -1) for a in arrays]
    both = jnp.concatenate(columns, axis=along)
    result, at, outs = (lax.psum_scatter(both, axis, scatter_dimension=dim, tiled=True), 0, [])
    for a, column in zip(arrays, columns):
        piece = result[..., at : at + column.shape[along]]
        outs.append(piece.reshape(*piece.shape[:along], *a.shape[along:]))
        at += column.shape[along]
    return tuple(outs)


def stored_positions(block_len, block_count):
    blocks = jnp.arange(block_count, dtype=jnp.int32)
    source = jnp.where(blocks % 2 == 0, blocks // 2, block_count - 1 - blocks // 2)
    return (source[:, None] * block_len + jnp.arange(block_len, dtype=jnp.int32)[None, :]).reshape(
        -1
    )


def angle_tables(positions):
    inverse = ROPE_BASE ** (-jnp.arange(0, HEAD_DIM // 2, dtype=jnp.float32) * 2.0 / HEAD_DIM)
    angles = positions.astype(jnp.float32)[:, None] * inverse[None, :]
    angles = jnp.concatenate([angles, angles], -1)
    return (jnp.cos(angles)[:, None, :], jnp.sin(angles)[:, None, :])


def rotate(values, cosines, sines):
    half_dim = values.shape[-1] // 2
    turned = jnp.concatenate([-values[..., half_dim:], values[..., :half_dim]], -1)
    return values * cosines + turned * sines


def rotate_back(grads, cosines, sines):
    half_dim = grads.shape[-1] // 2
    scaled = grads * sines
    return grads * cosines + jnp.concatenate([scaled[..., half_dim:], -scaled[..., :half_dim]], -1)


def contract_rows(left_side, right_side):
    return lax.dot_general(
        left_side, right_side, (((0,), (0,)), ((), ())), preferred_element_type=jnp.float32
    )


def times_transpose(left_side, right_side):
    return lax.dot_general(
        left_side, right_side, (((1,), (1,)), ((), ())), preferred_element_type=jnp.float32
    )


def norm_back(grad_normed, inputs, inv_rms, gain_full):
    scaled = grad_normed * gain_full
    return inv_rms * scaled - inputs * inv_rms**3 * jnp.mean(scaled * inputs, -1, keepdims=True)


def shards(
    tokens,
    segment_ids,
    cotangent,
    norm1_gain,
    q_weight,
    k_weight,
    v_weight,
    o_weight,
    norm2_gain,
    gate_weight,
    up_weight,
    down_weight,
):
    micro_count = tokens.shape[0]
    local_rows = tokens.shape[1]
    cp_count = lax.axis_size("cp")
    cp_index = lax.axis_index("cp")
    key_positions = stored_positions(local_rows // 2, 2 * cp_count)
    local_positions = lax.dynamic_slice_in_dim(key_positions, cp_index * local_rows, local_rows)
    cosines, sines = angle_tables(local_positions)
    local_heads = q_weight.shape[1] // HEAD_DIM
    local_kv = k_weight.shape[1] // HEAD_DIM
    group_size = local_heads // local_kv
    score_scale = HEAD_DIM ** (-0.5)
    all_ids = gather_directly(segment_ids, "cp", 1)
    full_rows = tokens.shape[2]
    acc_gain_one = jnp.zeros((full_rows,), jnp.float32)
    acc_query = jnp.zeros((full_rows, q_weight.shape[1]), jnp.float32)
    acc_key = jnp.zeros((full_rows, k_weight.shape[1]), jnp.float32)
    acc_value = jnp.zeros((full_rows, v_weight.shape[1]), jnp.float32)
    acc_output = jnp.zeros((full_rows, o_weight.shape[1]), jnp.float32)
    acc_gain_two = jnp.zeros((full_rows,), jnp.float32)
    acc_gate = jnp.zeros((full_rows, gate_weight.shape[1]), jnp.float32)
    acc_up = jnp.zeros((full_rows, up_weight.shape[1]), jnp.float32)
    acc_down = jnp.zeros((full_rows, down_weight.shape[1]), jnp.float32)
    outputs = []
    input_grads = []
    for micro_index in range(micro_count):
        attn_set = sent_together(
            (norm1_gain, q_weight, k_weight, v_weight, o_weight), ("fsdp", "cp"), 0, 1
        )
        gain_one, w_query, w_key, w_value, w_output = attn_set
        inputs = tokens[micro_index].astype(jnp.float32)
        inv_one = lax.rsqrt(jnp.mean(inputs * inputs, -1, keepdims=True) + NORM_EPS)
        normed = (inputs * inv_one * gain_one.astype(jnp.float32)).astype(jnp.bfloat16)
        q_pre = jnp.dot(normed, w_query, preferred_element_type=jnp.float32)
        k_pre = jnp.dot(normed, w_key, preferred_element_type=jnp.float32)
        v_pre = jnp.dot(normed, w_value, preferred_element_type=jnp.float32)
        queries = rotate(q_pre.reshape(local_rows, local_heads, HEAD_DIM), cosines, sines).astype(
            jnp.bfloat16
        )
        keys_rot = (
            rotate(k_pre.reshape(local_rows, local_kv, HEAD_DIM), cosines, sines)
            .astype(jnp.bfloat16)
            .reshape(local_rows, -1)
        )
        values_own = v_pre.astype(jnp.bfloat16)
        keys_all, values_all = side_by_side((keys_rot, values_own), "cp", 0, 1)
        total_rows = keys_all.shape[0]
        keys_all = keys_all.reshape(total_rows, local_kv, HEAD_DIM)
        values_all = values_all.reshape(total_rows, local_kv, HEAD_DIM)
        allowed = (segment_ids[micro_index][:, None] == all_ids[micro_index][None, :]) & (
            key_positions[None, :] <= local_positions[:, None]
        )
        grouped = queries.reshape(local_rows, local_kv, group_size, HEAD_DIM)
        scores = (
            jnp.einsum("rkgd,tkd->kgrt", grouped, keys_all, preferred_element_type=jnp.float32)
            * score_scale
        )
        scores = jnp.where(allowed, scores, -jnp.inf)
        row_top = jnp.max(scores, -1, keepdims=True)
        log_total = row_top + jnp.log(jnp.sum(jnp.exp(scores - row_top), -1, keepdims=True))
        probs_low = jnp.exp(scores - log_total).astype(jnp.bfloat16)
        mixed_heads = jnp.einsum(
            "kgrt,tkd->rkgd", probs_low, values_all, preferred_element_type=jnp.float32
        )
        attended = mixed_heads.reshape(local_rows, -1).astype(jnp.bfloat16)
        middle = inputs + over_copies(times_transpose(attended, w_output), "tp")
        mlp_set = sent_together(
            (norm2_gain, gate_weight, up_weight, down_weight), ("fsdp", "cp"), 0, 1
        )
        gain_two, w_gate, w_up, w_down = mlp_set
        inv_two = lax.rsqrt(jnp.mean(middle * middle, -1, keepdims=True) + NORM_EPS)
        normed_two = (middle * inv_two * gain_two.astype(jnp.float32)).astype(jnp.bfloat16)
        gate_pre = jnp.dot(normed_two, w_gate, preferred_element_type=jnp.float32)
        up_pre = jnp.dot(normed_two, w_up, preferred_element_type=jnp.float32)
        sigmoid_gate = jax.nn.sigmoid(gate_pre)
        hidden = (gate_pre * sigmoid_gate * up_pre).astype(jnp.bfloat16)
        result = middle + taken_together(
            times_transpose(hidden, w_down).astype(jnp.bfloat16), "tp"
        ).astype(jnp.float32)
        outputs.append(result.astype(jnp.bfloat16))
        mlp_back = sent_together(
            (norm2_gain, gate_weight, up_weight, down_weight), ("fsdp", "cp"), 0, 1
        )
        gain_two_b, gate_back, up_back, down_back = mlp_back
        grad_out = cotangent[micro_index].astype(jnp.float32)
        grad_branch = grad_out.astype(jnp.bfloat16)
        acc_down = acc_down + contract_rows(grad_branch, hidden)
        grad_hidden = jnp.dot(grad_branch, down_back, preferred_element_type=jnp.float32)
        grad_gate = (
            grad_hidden * up_pre * sigmoid_gate * (1.0 + gate_pre * (1.0 - sigmoid_gate))
        ).astype(jnp.bfloat16)
        grad_up = (grad_hidden * gate_pre * sigmoid_gate).astype(jnp.bfloat16)
        acc_gate = acc_gate + contract_rows(normed_two, grad_gate)
        acc_up = acc_up + contract_rows(normed_two, grad_up)
        grad_normed_two = over_copies(
            times_transpose(grad_gate, gate_back) + times_transpose(grad_up, up_back), "tp"
        )
        acc_gain_two = acc_gain_two + jnp.sum(grad_normed_two * middle * inv_two, 0)
        grad_middle = grad_out + norm_back(
            grad_normed_two, middle, inv_two, gain_two_b.astype(jnp.float32)
        )
        attn_back = sent_together(
            (norm1_gain, q_weight, k_weight, v_weight, o_weight), ("fsdp", "cp"), 0, 1
        )
        gain_one_b, query_back, key_back, value_back, output_back = attn_back
        grad_att = grad_middle.astype(jnp.bfloat16)
        acc_output = acc_output + contract_rows(grad_att, attended)
        grad_mixed = jnp.dot(grad_att, output_back, preferred_element_type=jnp.float32).astype(
            jnp.bfloat16
        )
        grad_mixed = grad_mixed.reshape(local_rows, local_kv, group_size, HEAD_DIM)
        scores = (
            jnp.einsum("rkgd,tkd->kgrt", grouped, keys_all, preferred_element_type=jnp.float32)
            * score_scale
        )
        scores = jnp.where(allowed, scores, -jnp.inf)
        probs_full = jnp.exp(scores - log_total)
        grad_probs = jnp.einsum(
            "rkgd,tkd->kgrt", grad_mixed, values_all, preferred_element_type=jnp.float32
        )
        grad_values = jnp.einsum(
            "kgrt,rkgd->tkd",
            probs_full.astype(jnp.bfloat16),
            grad_mixed,
            preferred_element_type=jnp.float32,
        )
        row_inner = jnp.sum(probs_full * grad_probs, -1, keepdims=True)
        grad_scores = (probs_full * (grad_probs - row_inner)).astype(jnp.bfloat16)
        grad_queries = (
            jnp.einsum("kgrt,tkd->rkgd", grad_scores, keys_all, preferred_element_type=jnp.float32)
            * score_scale
        )
        grad_keys = (
            jnp.einsum("kgrt,rkgd->tkd", grad_scores, grouped, preferred_element_type=jnp.float32)
            * score_scale
        )
        grad_keys_own, grad_values_own = tuple(
            (
                part.astype(jnp.float32)
                for part in in_one_piece(
                    (
                        grad_keys.reshape(total_rows, -1).astype(jnp.bfloat16),
                        grad_values.reshape(total_rows, -1).astype(jnp.bfloat16),
                    ),
                    "cp",
                    0,
                    1,
                )
            )
        )
        grad_q_pre = (
            rotate_back(grad_queries.reshape(local_rows, local_heads, HEAD_DIM), cosines, sines)
            .reshape(local_rows, -1)
            .astype(jnp.bfloat16)
        )
        grad_k_pre = (
            rotate_back(grad_keys_own.reshape(local_rows, local_kv, HEAD_DIM), cosines, sines)
            .reshape(local_rows, -1)
            .astype(jnp.bfloat16)
        )
        grad_v_pre = grad_values_own.astype(jnp.bfloat16)
        acc_query = acc_query + contract_rows(normed, grad_q_pre)
        acc_key = acc_key + contract_rows(normed, grad_k_pre)
        acc_value = acc_value + contract_rows(normed, grad_v_pre)
        grad_normed = taken_together(
            (
                times_transpose(grad_q_pre, query_back)
                + times_transpose(grad_k_pre, key_back)
                + times_transpose(grad_v_pre, value_back)
            ).astype(jnp.bfloat16),
            "tp",
        ).astype(jnp.float32)
        acc_gain_one = acc_gain_one + jnp.sum(grad_normed * inputs * inv_one, 0)
        grad_inputs = grad_middle + norm_back(
            grad_normed, inputs, inv_one, gain_one_b.astype(jnp.float32)
        )
        input_grads.append(grad_inputs.astype(jnp.bfloat16))
    attn_grads = side_by_side_2(
        (acc_gain_one, acc_query, acc_key, acc_value, acc_output), ("fsdp", "cp"), 0, 1
    )
    mlp_grads = side_by_side_2((acc_gain_two, acc_gate, acc_up, acc_down), ("fsdp", "cp"), 0, 1)
    return (
        jnp.stack(outputs),
        jnp.stack(input_grads),
        attn_grads[0],
        attn_grads[1],
        attn_grads[2],
        attn_grads[3],
        attn_grads[4],
        mlp_grads[0],
        mlp_grads[1],
        mlp_grads[2],
        mlp_grads[3],
    )


def solution(mesh):
    return jax.shard_map(
        shards,
        mesh=mesh,
        in_specs=(
            P("fsdp", "cp", None),
            P("fsdp", "cp"),
            P("fsdp", "cp", None),
            P(("fsdp", "cp")),
            P(("fsdp", "cp"), "tp"),
            P(("fsdp", "cp"), "tp"),
            P(("fsdp", "cp"), "tp"),
            P(("fsdp", "cp"), "tp"),
            P(("fsdp", "cp")),
            P(("fsdp", "cp"), "tp"),
            P(("fsdp", "cp"), "tp"),
            P(("fsdp", "cp"), "tp"),
        ),
        out_specs=(
            P("fsdp", "cp", None),
            P("fsdp", "cp", None),
            P(("fsdp", "cp")),
            P(("fsdp", "cp"), "tp"),
            P(("fsdp", "cp"), "tp"),
            P(("fsdp", "cp"), "tp"),
            P(("fsdp", "cp"), "tp"),
            P(("fsdp", "cp")),
            P(("fsdp", "cp"), "tp"),
            P(("fsdp", "cp"), "tp"),
            P(("fsdp", "cp"), "tp"),
        ),
        check_vma=False,
    )
```

profile of v0, /device:TPU:0, one launch (start us, length us, event | category | flops | bytes accessed | tf_op | source)
XLA Modules:
  0.0 3598.3 jit_solution(17300710222311740594)
XLA Ops:
  14.0 7.0 all-to-all-start
  23.9 4.8 all-to-all-done
  29.4 350.6 %all-gather.3.cloned.1.call-done = bf16[2048,2305]{1,0:T(8,128)(2,1)} async-done(((bf16[32,2305]{1,0:T(8,128)(2,1)}), bf16[2048,2305]{1,0:T(8,128)(2,1)}) %all-gather.3.cloned.1.call-update) | async-done | bytes 9441296 | tf_op jit(solution)/shard_map/all_gather | solution.py:36
  381.7 6.6 slice_bitcast_fusion
  388.3 6.5 copy.95
  398.5 34.5 all_gather.9
  433.0 3.7 fusion.149
  441.9 4.6 fusion.50
  446.7 6.4 all_to_all.45
  458.2 34.3 all_gather.21
  492.5 3.7 fusion.144
  501.4 4.6 fusion.48
  506.2 6.3 all_to_all.46
  512.5 2.8 reduce_sum.241
  516.9 646.0 %all-gather.5.cloned.1.call-done = bf16[2048,8449]{1,0:T(8,128)(2,1)} async-done(((bf16[32,8449]{1,0:T(8,128)(2,1)}), bf16[2048,8449]{1,0:T(8,128)(2,1)}) %all-gather.5.cloned.1.call-update) | async-done | bytes 34607120 | tf_op jit(solution)/shard_map/all_gather | solution.py:36
  1165.8 8.5 fusion.37
  1174.3 8.0 fusion.20
  1182.3 9.8 multiply_convert_fusion.3
  1192.1 7.9 fusion.16
  1200.0 7.4 fusion.52
  1209.0 4.8 all-to-all-start.5
  1213.8 8.2 fusion.34
  1222.0 8.0 fusion.18
  1230.0 9.6 multiply_convert_fusion.1
  1240.6 7.8 fusion.14
  1248.4 9.5 fusion.55
  1257.9 2.8 broadcast_in_dim.83
  1260.8 4.8 all-to-all-start.7
  1265.6 2.9 reduce_sum.246
  1268.6 2.8 reduce_sum.253
  1273.9 4.6 fusion.80
  1278.7 6.1 fusion.78
  1284.8 7.0 fusion.3
  1291.9 4.1 fusion.83
  1296.9 6.2 fusion.79
  1303.1 9.1 fusion
  1312.2 13.1 fusion.2
  1325.4 4.5 fusion.87
  1329.9 3.2 convolution_multiply_fusion
  1335.3 8.3 fusion.60
  1344.8 4.4 all-to-all-start.2
  1357.6 4.6 fusion.153
  1364.1 8.6 fusion.63
  1373.9 4.0 all-to-all-start.4
  1380.5 5.6 fusion.42
  1387.2 4.5 fusion.40
  1391.7 8.0 convolution_add_fusion.3
  1399.7 21.6 reduce-scatter.15.cloned.1.call-done
  1422.3 72.1 %reduce-scatter.13.cloned.1.call-done = bf16[128,256]{1,0:T(8,128)(2,1)} async-done(((bf16[1024,256]{1,0:T(8,128)(2,1)}), bf16[128,256]{1,0:T(8,128)(2,1)}) %reduce-scatter.13.cloned.1.call-update) | async-done | bytes 65552
  1501.6 4.4 all-to-all-start.6
  1510.6 4.4 all-to-all-start.8
  1523.9 3.7 fusion.99
  1530.7 4.6 convolution_add_fusion.2
  1537.1 52.7 %concatenate.92 = f32[2048,2305]{0,1:T(8,128)} concatenate(f32[2048,1]{0,1:T(1,128)S(1)} %bitcast.463, f32[2048,1024]{0,1:T(8,128)} %convolution_add_fusion.3, f32[2048,128]{0,1:T(8,128)S(1)} %copy-done.16, f32[2048,128]{0,1:T(8,128)} %convolution_add_fusion.4, f32[2048,1024]{0,1:T(8,128)} %convolution_add_fusion.2), dimensions={1} | concatenate | bytes 37765120 | tf_op jit(solution)/shard_map/concatenate | solution.py:70
  1589.8 19.7 copy.140
  1611.0 9.6 fusion.140
  1620.5 9.3 fusion.233
  1629.9 9.5 fusion.234
  1639.4 15.1 add_bitcast_fusion
  1654.5 15.0 convolution_add_fusion.1
  1669.6 15.1 convolution_add_fusion
  1684.7 87.6 %concatenate.93 = f32[2048,8449]{1,0:T(8,128)} concatenate(f32[2048,1]{1,0:T(8,128)S(1)} %copy.111, f32[2048,2816]{1,0:T(8,128)} %convolution_add_fusion.1, f32[2048,2816]{1,0:T(8,128)} %convolution_add_fusion, f32[2048,2816]{1,0:T(8,128)} %add_bitcast_fusion), dimensions={1} | concatenate | bytes 138428416 | tf_op jit(solution)/shard_map/concatenate | solution.py:70
  1775.6 311.4 %reduce-scatter.17.cloned.1.call-done = f32[32,2305]{1,0:T(8,128)} async-done(((f32[2048,2305]{1,0:T(8,128)}), f32[32,2305]{1,0:T(8,128)}) %reduce-scatter.17.cloned.1.call-update) | async-done | bytes 295056
  2091.7 1495.7 %reduce-scatter.11.cloned.1.call-done = f32[32,8449]{1,0:T(8,128)} async-done(((f32[2048,8449]{1,0:T(8,128)}), f32[32,8449]{1,0:T(8,128)}) %reduce-scatter.11.cloned.1.call-update) | async-done | bytes 1081488 | tf_op jit(solution)/shard_map/reduce_scatter | solution.py:71
  (246 shorter events, 99.9 us)
Async XLA Ops:
  7.2 372.9 %all-gather.3.cloned.1.call-start = ((), (), s32[]{:S(2)}) async-start(), calls=%async_computation.13 | async-start | bytes 10117120 | tf_op jit(solution)/shard_map/all_gather | solution.py:36
  9.7 1153.1 %all-gather.5.cloned.1.call-start = ((), (), s32[]{:S(2)}) async-start(), calls=%async_computation.14 | async-start | bytes 35676160 | tf_op jit(solution)/shard_map/all_gather | solution.py:36
  14.0 14.7 all-to-all-start
  381.7 14.4 copy-start.2
  433.0 5.2 copy-start.20
  433.0 6.9 copy-start.34
  438.2 3.6 copy-start
  441.9 13.4 copy-start.45
  454.9 819.0 %copy-start.4 = (f32[128,2048]{1,0:T(8,128)}, f32[128,2048]{1,0:T(8,128)S(1)}, u32[]{:S(2)}) copy-start(f32[128,2048]{1,0:T(8,128)S(1)} %reduce_sum.234) | copy-start | bytes 3145732
  492.5 5.2 copy-start.24
  492.5 6.9 copy-start.36
  496.4 1.4 copy-start.25
  497.7 3.6 copy-start.1
  501.4 15.5 copy-start.47
  1165.7 16.6 copy-start.13
  1165.7 64.3 %copy-start.8 = (bf16[128,2048]{1,0:T(8,128)(2,1)}, bf16[128,2048]{1,0:T(8,128)(2,1)S(1)}, u32[]{:S(2)}) copy-start(bf16[128,2048]{1,0:T(8,128)(2,1)S(1)} %get-tuple-element.87) | copy-start | bytes 1572868
  1192.1 7.9 copy-start.37
  1192.1 15.3 copy-start.39
  1209.0 48.9 %all-to-all-start.5 = ((f32[2,128,2048]{2,1,0:T(8,128)}), f32[2,128,2048]{2,1,0:T(8,128)}, u32[]{:S(2)}, u32[]{:S(2)}) async-start(f32[2,128,2048]{2,1,0:T(8,128)} %broadcast_in_dim.42), calls=%async_computation.5 | async-start | bytes 4194304 | tf_op jit(solution)/shard_map/all_to_all | solution.py:17
  1239.7 8.7 copy-start.43
  1260.8 7.8 all-to-all-start.7
  1273.9 10.9 copy-start.35
  1284.8 7.0 copy-start.6
  1284.8 7.0 copy-start.10
  1284.8 7.0 copy-start.17
  1296.9 15.3 slice-start
  1303.1 9.1 slice-start.1
  1325.3 7.7 copy-start.3
  1325.3 7.7 copy-start.23
  1325.3 9.1 copy-start.21
  1329.9 5.4 copy-start.31
  1343.6 9.7 copy-start.49
  1344.8 28.0 all-to-all-start.2
  1349.2 72.1 %reduce-scatter.15.cloned.1.call-start = ((), (), s32[]{:S(2)}) async-start(), calls=%async_computation.17 | async-start | bytes 589824
  1351.3 143.1 %reduce-scatter.13.cloned.1.call-start = ((), (), s32[]{:S(2)}) async-start(), calls=%async_computation.16 | async-start | bytes 589824
  1364.1 16.3 copy-start.50
  1373.9 12.1 all-to-all-start.4
  1421.3 86.4 %copy-start.51 = (bf16[128,256]{1,0:T(8,128)(2,1)S(1)}, bf16[128,256]{1,0:T(8,128)(2,1)}, u32[]{:S(2)}) copy-start(bf16[128,256]{1,0:T(8,128)(2,1)} %reduce-scatter.15.cloned.1.call-done) | copy-start | bytes 196612
  1501.6 7.9 all-to-all-start.6
  1507.7 16.1 copy-start.5
  1507.7 16.1 copy-start.53
  1510.6 7.2 all-to-all-start.8
  1515.0 12.6 copy-start.46
  1515.0 572.1 %reduce-scatter.17.cloned.1.call-start = ((), (), s32[]{:S(2)}) async-start(), calls=%async_computation.18 | async-start | bytes 20234240
  1517.7 6.1 copy-start.12
  1523.8 5.0 copy-start.7
  1523.8 5.0 copy-start.11
  1523.9 5.0 copy-start.15
  1523.9 5.0 copy-start.18
  1523.9 5.0 copy-start.54
  1527.5 3.1 copy-start.48
  1530.7 4.6 copy-start.52
  1530.7 6.4 copy-start.16
  1609.5 1.4 copy-start.32
  1609.5 1977.8 %reduce-scatter.11.cloned.1.call-start = ((), (), s32[]{:S(2)}) async-start(), calls=%async_computation.15 | async-start | bytes 71352320 | tf_op jit(solution)/shard_map/reduce_scatter | solution.py:71
  1610.9 9.6 copy-start.14
  1610.9 9.6 copy-start.40
  1620.5 9.3 copy-start.38
  1629.9 9.5 copy-start.30
  1639.4 15.1 copy-start.9
  1639.4 15.1 copy-start.44
  1654.5 15.0 copy-start.42
  1772.3 2.3 copy-start.26
  1772.3 2.3 copy-start.28
  (6 other events, 6.5 us)
Sparse Core Ops, SparseCore 0:
  10.2 369.7 all-gather.2
  382.2 780.5 all-gather.4
  1353.6 67.7 reduce-scatter.14
  1425.1 69.2 reduce-scatter.12
  1609.7 477.3 reduce-scatter.16
  2089.5 1497.8 reduce-scatter.10
where the time goes:
time: 3610 us; the launch traced here: 3600 us
  waiting for transfers between devices  2900 us (80%)
  matrix products  292 us (8%)
  local copies, waits for them, and re-layouts  209 us (6%)
  blocking collectives  81.4 us (2%)
  other arithmetic  64.1 us (2%)
    reduce_scatter x1, waiting for transfers between devices, side_by_side_2(): lax.psum_scatter(both, axis, scatter_dimension=dim, tiled=True)  1500 us
    all_gather x2, waiting for transfers between devices, sent_together(): result = lax.all_gather(both, axis, axis=dim, tiled=True)  997 us
    unnamed x9, waiting for transfers between devices  405 us
    concatenate x2, local copies, waits for them, and re-layouts, side_by_side_2(): both = jnp.concatenate(columns, axis=along)  140 us
    dot_general x14, matrix products, contract_rows(): lax.dot_general(left_side, right_side, (((0,), (0,)), ((), ())), preferre...  97.9 us
    dot_general x14, matrix products, times_transpose(): lax.dot_general(left_side, right_side, (((1,), (1,)), ((), ())), preferre...  75.9 us
  transfers between devices with their start and end apart: 13, of which 8 were waited for; matrix products, arithmetic and copies ran while one was open for 9% of the time, Pallas kernels for 0%

commit v1 on v0

v1 whole, which is shorter than its diff:
```python
import jax
import jax.numpy as jnp
from jax import lax
from jax.experimental import pallas as pl
from jax.experimental.pallas import tpu as pltpu
from jax.sharding import Mesh
from jax.sharding import PartitionSpec as P

HEAD_DIM = 64
NORM_EPS = 1e-05
ROPE_BASE = 10000.0
X_RING = ("xl", "xh")
OFFSETS = (0, -1, 1, 2)
bf16 = jnp.bfloat16
f32 = jnp.float32


def x_index(x):
    return (x % 2) * 2 + x // 2


def shift(v, ring, d):
    if ring == X_RING:
        return lax.ppermute(v, X_RING, [(x_index(i), x_index((i + d) % 4)) for i in range(4)])
    n = 2 if ring in ("c", "xh") else 4
    return lax.ppermute(v, ring, [(i, (i + d) % n) for i in range(n)])


def ring_gather(v, ring):
    half = v.shape[0] // 2
    left = shift(v, ring, 1)
    right = shift(v, ring, -1)
    far_a = shift(left[:half], ring, 1)
    far_b = shift(right[half:], ring, -1)
    return v, left, right, jnp.concatenate([far_a, far_b], 0)


def ring_scatter(own, left, right, far, ring):
    half = far.shape[0] // 2
    a = shift(far[:half], ring, 1)
    b = shift(far[half:], ring, -1)
    up = jnp.concatenate([(right[:half].astype(f32) + a.astype(f32)).astype(bf16), right[half:]], 0)
    down = jnp.concatenate([left[:half], (left[half:].astype(f32) + b.astype(f32)).astype(bf16)], 0)
    u = shift(up, ring, 1)
    d = shift(down, ring, -1)
    return own.astype(f32) + u.astype(f32) + d.astype(f32)


def gather_rows(block, first):
    z = lax.axis_index("z")
    xl = lax.axis_index("xl")
    xh = lax.axis_index("xh")
    x = xh * 2 + xl
    n = block.shape[-1]
    out = jnp.zeros((4, 2, 4, 2, 32, n), block.dtype)
    if first == "z":
        mid = jnp.zeros((4, 4, 32, n), block.dtype)
        for off, part in zip(OFFSETS, ring_gather(block, "z")):
            mid = lax.dynamic_update_slice(mid, part[None], ((z + off) % 4, 0, 0, 0))
        for off, part in zip(OFFSETS, ring_gather(mid, X_RING)):
            xj = (x + off) % 4
            out = lax.dynamic_update_slice(
                out, part[:, None, :, None], (0, xj % 2, 0, xj // 2, 0, 0)
            )
    else:
        mid = jnp.zeros((2, 4, 2, 32, n), block.dtype)
        for off, part in zip(OFFSETS, ring_gather(block, X_RING)):
            xj = (x + off) % 4
            mid = lax.dynamic_update_slice(
                mid, part[None, :, None], (xj % 2, 0, xj // 2, 0, 0)
            )
        for off, part in zip(OFFSETS, ring_gather(mid, "z")):
            out = lax.dynamic_update_slice(out, part[None], ((z + off) % 4, 0, 0, 0, 0, 0))
    return out.reshape(2048, n)


def scatter_rows(grad, first):
    z = lax.axis_index("z")
    xl = lax.axis_index("xl")
    xh = lax.axis_index("xh")
    x = xh * 2 + xl
    n = grad.shape[-1]
    g = grad.reshape(4, 2, 4, 2, 32, n)
    if first == "x":
        parts = []
        for off in OFFSETS:
            xj = (x + off) % 4
            parts.append(
                lax.dynamic_slice(g, (0, xj % 2, 0, xj // 2, 0, 0), (4, 1, 4, 1, 32, n)).reshape(4, 4, 32, n)
            )
        g = ring_scatter(*parts, X_RING).astype(bf16)
        parts = [lax.dynamic_index_in_dim(g, (z + off) % 4, 0, False) for off in OFFSETS]
        return ring_scatter(*parts, "z").astype(bf16)
    parts = [lax.dynamic_index_in_dim(g, (z + off) % 4, 0, False) for off in OFFSETS]
    g = ring_scatter(*parts, "z").astype(bf16)
    parts = []
    for off in OFFSETS:
        xj = (x + off) % 4
        parts.append(lax.dynamic_slice(g, (xj % 2, 0, xj // 2, 0, 0), (1, 4, 1, 32, n)).reshape(4, 32, n))
    return ring_scatter(*parts, X_RING).astype(bf16)


def positions_of(y, xh):
    rows = []
    o = jnp.arange(64, dtype=jnp.int32)
    for off in OFFSETS:
        i = ((y + off) % 4) * 2 + xh
        rows += [i * 64 + o, (15 - i) * 64 + o]
    return jnp.concatenate(rows)


def rope_tables(positions, heads):
    inverse = ROPE_BASE ** (-jnp.arange(0, HEAD_DIM // 2, dtype=f32) * 2.0 / HEAD_DIM)
    angles = positions.astype(f32)[:, None] * inverse[None, :]
    cos = jnp.cos(angles)
    sin = jnp.sin(angles)
    cos = jnp.tile(jnp.concatenate([cos, cos], -1), (1, heads))
    sin = jnp.tile(jnp.concatenate([-sin, sin], -1), (1, heads))
    return cos, sin


def swap_halves(u):
    lane = lax.broadcasted_iota(jnp.int32, u.shape, 1)
    return jnp.where(lane % HEAD_DIM < HEAD_DIM // 2, jnp.roll(u, -32, 1), jnp.roll(u, 32, 1))


def rotate(u, cos, sin):
    w = u.shape[1]
    return u * cos[:, :w] + swap_halves(u) * sin[:, :w]


def rotate_back(w, cos, sin):
    n = w.shape[1]
    return w * cos[:, :n] + swap_halves(w * sin[:, :n])


def dot(a, b):
    return jnp.dot(a, b, preferred_element_type=f32)


def dot_nt(a, b):
    return lax.dot_general(a, b, (((1,), (1,)), ((), ())), preferred_element_type=f32)


def dot_tn(a, b):
    return lax.dot_general(a, b, (((0,), (0,)), ((), ())), preferred_element_type=f32)


def mask_of(qpos, qseg, kpos, kseg):
    return jnp.where((qseg == kseg) & (kpos <= qpos), 0.0, -jnp.inf).astype(f32)


def attend_kernel(q_ref, kv_ref, kv2_ref, qpos_ref, qseg_ref, kpos_ref, kseg_ref, out_ref, log_ref):
    mask = mask_of(qpos_ref[...], qseg_ref[...], kpos_ref[...], kseg_ref[...])
    outs, logs = [], []
    for g in range(2):
        keys = jnp.concatenate([kv_ref[:, g * 64 : g * 64 + 64], kv2_ref[:, g * 64 : g * 64 + 64]], 0)
        values = jnp.concatenate(
            [kv_ref[:, 128 + g * 64 : 192 + g * 64], kv2_ref[:, 128 + g * 64 : 192 + g * 64]], 0
        )
        for h in range(4):
            at = (g * 4 + h) * 64
            s = dot_nt(q_ref[:, at : at + 64] * jnp.asarray(0.125, bf16), keys) + mask
            top = jnp.max(s, -1, keepdims=True)
            p = jnp.exp(s - top)
            total = jnp.sum(p, -1, keepdims=True)
            outs.append(dot(p.astype(bf16), values) / total)
            logs.append(top + jnp.log(total))
    out_ref[...] = jnp.concatenate(outs, 1).astype(bf16)
    log_ref[...] = jnp.concatenate(logs, 1)


def attend(q, kv, kv2, qpos, qseg, kpos, kseg):
    tile = 128
    rows = q.shape[0]
    whole = lambda a: pl.BlockSpec(a.shape, lambda i: (0, 0))
    tiled = lambda a: pl.BlockSpec((tile, a.shape[1]), lambda i: (i, 0))
    return pl.pallas_call(
        attend_kernel,
        grid=(rows // tile,),
        in_specs=[tiled(q), whole(kv), whole(kv2), tiled(qpos), tiled(qseg), whole(kpos), whole(kseg)],
        out_specs=[tiled(q), pl.BlockSpec((tile, 8), lambda i: (i, 0))],
        out_shape=[
            jax.ShapeDtypeStruct(q.shape, bf16),
            jax.ShapeDtypeStruct((rows, 8), f32),
        ],
        compiler_params=pltpu.CompilerParams(vmem_limit_bytes=40 << 20),
        cost_estimate=pl.CostEstimate(flops=2 << 30, bytes_accessed=2 << 20, transcendentals=4 << 20),
        name="attend",
    )(q, kv, kv2, qpos, qseg, kpos, kseg)


def attend_back_kernel(
    q_ref, g_ref, log_ref, kv_ref, kv2_ref, qpos_ref, qseg_ref, kpos_ref, kseg_ref, dq_ref, dkv_ref, dkv2_ref
):
    @pl.when(pl.program_id(0) == 0)
    def _():
        dkv_ref[...] = jnp.zeros_like(dkv_ref)
        dkv2_ref[...] = jnp.zeros_like(dkv2_ref)

    mask = mask_of(qpos_ref[...], qseg_ref[...], kpos_ref[...], kseg_ref[...])
    half = kv_ref.shape[0]
    for g in range(2):
        keys = jnp.concatenate([kv_ref[:, g * 64 : g * 64 + 64], kv2_ref[:, g * 64 : g * 64 + 64]], 0)
        values = jnp.concatenate(
            [kv_ref[:, 128 + g * 64 : 192 + g * 64], kv2_ref[:, 128 + g * 64 : 192 + g * 64]], 0
        )
        dk = jnp.zeros((2 * half, 64), f32)
        dv = jnp.zeros((2 * half, 64), f32)
        for h in range(4):
            at = (g * 4 + h) * 64
            q = q_ref[:, at : at + 64] * jnp.asarray(0.125, bf16)
            grad = g_ref[:, at : at + 64]
            s = dot_nt(q, keys) + mask
            p = jnp.exp(s - log_ref[:, g * 4 + h : g * 4 + h + 1])
            dp = dot_nt(grad, values)
            t = p * dp
            ds = (t - p * jnp.sum(t, -1, keepdims=True)).astype(bf16)
            dq_ref[:, at : at + 64] = dot(ds, keys) * 0.125
            dk += dot_tn(ds, q)
            dv += dot_tn(p.astype(bf16), grad)
        dkv_ref[:, g * 64 : g * 64 + 64] += dk[:half]
        dkv2_ref[:, g * 64 : g * 64 + 64] += dk[half:]
        dkv_ref[:, 128 + g * 64 : 192 + g * 64] += dv[:half]
        dkv2_ref[:, 128 + g * 64 : 192 + g * 64] += dv[half:]


def attend_back(q, grad, logs, kv, kv2, qpos, qseg, kpos, kseg):
    tile = 128
    rows = q.shape[0]
    whole = lambda a: pl.BlockSpec(a.shape, lambda i: (0, 0))
    tiled = lambda a: pl.BlockSpec((tile, a.shape[1]), lambda i: (i, 0))
    return pl.pallas_call(
        attend_back_kernel,
        grid=(rows // tile,),
        in_specs=[
            tiled(q),
            tiled(grad),
            tiled(logs),
            whole(kv),
            whole(kv2),
            tiled(qpos),
            tiled(qseg),
            whole(kpos),
            whole(kseg),
        ],
        out_specs=[tiled(q), whole(kv), whole(kv)],
        out_shape=[
            jax.ShapeDtypeStruct(q.shape, f32),
            jax.ShapeDtypeStruct(kv.shape, f32),
            jax.ShapeDtypeStruct(kv.shape, f32),
        ],
        compiler_params=pltpu.CompilerParams(vmem_limit_bytes=48 << 20),
        cost_estimate=pl.CostEstimate(flops=5 << 30, bytes_accessed=4 << 20, transcendentals=4 << 20),
        name="attend_back",
    )(q, grad, logs, kv, kv2, qpos, qseg, kpos, kseg)


def inverse_rms(v):
    return lax.rsqrt(jnp.mean(v * v, -1, keepdims=True) + NORM_EPS)


def norm_back(grad_normed, inputs, inv_rms, gain):
    scaled = grad_normed * gain
    return inv_rms * scaled - inputs * inv_rms**3 * jnp.mean(scaled * inputs, -1, keepdims=True)


def blocks(v):
    return tuple(v[k * 128 : (k + 1) * 128] for k in range(4))


def layer(
    tokens,
    segment_ids,
    cotangent,
    norm1_gain,
    q_weight,
    k_weight,
    v_weight,
    o_weight,
    norm2_gain,
    gate_weight,
    up_weight,
    down_weight,
):
    y = lax.axis_index("y")
    xh = lax.axis_index("xh")
    core = lax.axis_index("c")
    own = lambda a: lax.dynamic_index_in_dim(a, core, 0, False)
    x_own = own(tokens)
    ct_own = own(cotangent)

    gains = lax.all_gather(
        jnp.stack([norm1_gain, norm2_gain], 0), ("z", "xl", "y", "xh"), axis=1, tiled=True
    ).astype(f32)

    def per_chip(*arrays):
        joined = jnp.concatenate([a.reshape(32, 4, -1) for a in arrays], -1)
        return lax.all_to_all(joined.transpose(1, 0, 2), "y", 0, 0, tiled=True)

    twice = lambda a: jnp.repeat(a.reshape(32, 2, 64), 2, axis=1)
    attn_block = per_chip(q_weight, twice(k_weight), twice(v_weight), o_weight)
    x_all = jnp.concatenate(ring_gather(x_own, "y"), 0)
    seg_all = jnp.concatenate(ring_gather(own(segment_ids)[:, None], "y"), 0)
    w_qkv = gather_rows(attn_block[:, :, :384], "z")
    w_o = gather_rows(attn_block[:, :, 384:], "x")
    w_qkv2 = shift(w_qkv, "c", 1)
    w_o2 = shift(w_o, "c", 1)

    gu_block = per_chip(gate_weight, up_weight)
    down_block = per_chip(down_weight)
    ct_all = jnp.concatenate(ring_gather(ct_own, "y"), 0)
    w_gu = gather_rows(gu_block, "z")
    w_down = gather_rows(down_block, "x")
    w_gu2 = shift(w_gu, "c", 1)
    w_down2 = shift(w_down, "c", 1)

    qpos = positions_of(y, xh)
    kpos = jnp.concatenate([qpos, positions_of(y, 1 - xh)])
    cos, sin = rope_tables(qpos, 4)
    x_f = x_all.astype(f32)
    inv_one = inverse_rms(x_f)
    h1 = (x_f * inv_one * gains[0]).astype(bf16)

    def project(w):
        pre = dot(h1, w)
        return (
            rotate(pre[:, :256], cos, sin).astype(bf16),
            rotate(pre[:, 256:320], cos, sin).astype(bf16),
            pre[:, 320:].astype(bf16),
        )

    q_a, k_a, v_a = project(w_qkv)
    q_b, k_b, v_b = project(w_qkv2)
    queries = jnp.concatenate([q_a, q_b], 1)
    kv = jnp.concatenate([k_a, k_b, v_a, v_b], 1)
    kv2 = shift(kv, "xh", 1)
    seg2 = shift(seg_all, "xh", 1)
    qp = qpos[:, None]
    kp = kpos[None, :]
    kseg = jnp.concatenate([seg_all, seg2], 0).reshape(1, -1)
    attended, logs = attend(queries, kv, kv2, qp, seg_all, kp, kseg)
    o_part = (dot_nt(attended[:, :256], w_o) + dot_nt(attended[:, 256:], w_o2)).astype(bf16)
    middle = x_own.astype(f32) + ring_scatter(*blocks(o_part), "y")

    inv_two = inverse_rms(middle)
    h2_own = (middle * inv_two * gains[1]).astype(bf16)
    h2 = jnp.concatenate(ring_gather(h2_own, "y"), 0)

    def hidden_of(w_gu_s, w_down_s):
        pre = dot(h2, w_gu_s)
        gate, up = pre[:, :704], pre[:, 704:]
        sig = jax.nn.sigmoid(gate)
        hidden = (gate * sig * up).astype(bf16)
        d_hidden = dot(ct_all, w_down_s)
        d_gate = (d_hidden * up * sig * (1.0 + gate * (1.0 - sig))).astype(bf16)
        d_up = (d_hidden * gate * sig).astype(bf16)
        return hidden, jnp.concatenate([d_gate, d_up], 1)

    hid_a, d_gu_a = hidden_of(w_gu, w_down)
    hid_b, d_gu_b = hidden_of(w_gu2, w_down2)
    d_h2_part = (dot_nt(d_gu_a, w_gu) + dot_nt(d_gu_b, w_gu2)).astype(bf16)
    out_part = (dot_nt(hid_a, w_down) + dot_nt(hid_b, w_down2)).astype(bf16)
    d_h2 = ring_scatter(*blocks(d_h2_part), "y")
    g_down = dot_tn(ct_all, hid_a) + shift(dot_tn(ct_all, hid_b).astype(bf16), "c", 1).astype(f32)
    g_gu = dot_tn(h2, d_gu_a) + shift(dot_tn(h2, d_gu_b).astype(bf16), "c", 1).astype(f32)
    gain_two_grad = jnp.sum(d_h2 * middle * inv_two, 0)
    d_middle = ct_own.astype(f32) + norm_back(d_h2, middle, inv_two, gains[1])
    da_own = d_middle.astype(bf16)
    da = jnp.concatenate(ring_gather(da_own, "y"), 0)
    out_own = (middle + ring_scatter(*blocks(out_part), "y")).astype(bf16)

    g_o = dot_tn(da, attended[:, :256]) + shift(
        dot_tn(da, attended[:, 256:]).astype(bf16), "c", 1
    ).astype(f32)
    d_att = jnp.concatenate([dot(da, w_o), dot(da, w_o2)], 1).astype(bf16)
    d_q, d_kv, d_kv2 = attend_back(queries, d_att, logs, kv, kv2, qp, seg_all, kp, kseg)
    d_kv = d_kv + shift(d_kv2.astype(bf16), "xh", 1).astype(f32)
    dq_a = rotate_back(d_q[:, :256], cos, sin)
    dq_b = rotate_back(d_q[:, 256:], cos, sin)
    dk = rotate_back(d_kv[:, :128], cos, sin)
    d_a = jnp.concatenate([dq_a, dk[:, :64], d_kv[:, 128:192]], 1).astype(bf16)
    d_b = jnp.concatenate([dq_b, dk[:, 64:], d_kv[:, 192:]], 1).astype(bf16)
    d_h1_full = dot_nt(d_a, w_qkv) + dot_nt(d_b, w_qkv2)
    gain_one_grad = jnp.sum(d_h1_full * x_f * inv_one, 0)
    d_h1 = ring_scatter(*blocks(d_h1_full.astype(bf16)), "y")
    g_qkv = dot_tn(h1, d_a) + shift(dot_tn(h1, d_b).astype(bf16), "c", 1).astype(f32)
    dx_own = (d_middle + norm_back(d_h1, x_own.astype(f32), inv_one[:128], gains[0])).astype(bf16)

    def to_owner(grad, first):
        part = scatter_rows(grad.astype(bf16), first)
        got = lax.all_to_all(part, "y", 0, 0, tiled=True)
        return got.astype(f32)

    def columns(got):
        return got.transpose(1, 0, 2).reshape(32, -1)

    own_down = to_owner(g_down, "z")
    own_gu = to_owner(g_gu, "x")
    own_o = to_owner(g_o, "z")
    own_qkv = to_owner(g_qkv, "x")
    gain_grads = jnp.stack([gain_one_grad, gain_two_grad], 0).reshape(2, 64, 32).transpose(1, 0, 2)
    gain_got = lax.all_to_all(gain_grads, ("z", "xl", "y", "xh"), 0, 0, tiled=True).sum(0)
    gain_got = gain_got + shift(gain_got, "c", 1)

    pair = lambda a: a.reshape(2, 2, 32, 64).sum(1).transpose(1, 0, 2).reshape(32, 128)

    def both(a):
        other = shift(a, "c", 1)
        return jnp.where(core == 0, jnp.stack([a, other]), jnp.stack([other, a]))

    return (
        both(out_own),
        both(dx_own),
        gain_got[0],
        columns(own_qkv[:, :, :256]),
        pair(own_qkv[:, :, 256:320]),
        pair(own_qkv[:, :, 320:]),
        columns(own_o),
        gain_got[1],
        columns(own_gu[:, :, :704]),
        columns(own_gu[:, :, 704:]),
        columns(own_down),
    )


def solution(mesh):
    fine = Mesh(mesh.devices.reshape(4, 2, 4, 2, 2), ("z", "xl", "y", "xh", "c"))
    fsdp, cp = ("z", "xl"), ("y", "xh")
    acts, gain, weight = P(fsdp, cp, None), P(fsdp + cp), P(fsdp + cp, "c")
    return jax.shard_map(
        layer,
        mesh=fine,
        in_specs=(acts, P(fsdp, cp), acts, gain, weight, weight, weight, weight, gain, weight, weight, weight),
        out_specs=(acts, acts, gain, weight, weight, weight, weight, gain, weight, weight, weight),
        check_vma=False,
    )
```

time: 3610 us -> 795 us (0.22)
  waiting for transfers between devices: 2900 us -> 181 us
  matrix products: 292 us -> 79.9 us
  starting transfers between devices: 34.8 us -> 186 us
  local copies, waits for them, and re-layouts: 209 us -> 80.4 us
  blocking collectives: 81.4 us -> 176 us
    reduce_scatter x1 -> x0, waiting for transfers between devices: 1500 us -> none  [side_by_side_2(): lax.psum_scatter(both, axis, scatter_dimension=dim, tiled=True)]
    all_gather x2 -> x0, waiting for transfers between devices: 997 us -> none  [sent_together(): result = lax.all_gather(both, axis, axis=dim, tiled=True)]
    unnamed x9 -> x0, waiting for transfers between devices: 405 us -> none
    dot_general x54 -> x24, matrix products: 292 us -> 79.9 us  [the longest x8 29 us: dot_tn(): lax.dot_general(a, b, (((0,), (0,)), ((), ())), preferred_element_type=f32)]
    ppermute x0 -> x114, waiting for transfers between devices: none -> 160 us  [the longest x82 86.3 us: shift(): return lax.ppermute(v, ring, [(i, (i + d) % n) for i in range(n)])]
    ppermute x0 -> x114, starting transfers between devices: none -> 154 us  [the longest x82 103 us: shift(): return lax.ppermute(v, ring, [(i, (i + d) % n) for i in range(n)])]
    concatenate x4 -> x9, local copies, waits for them, and re-layouts: 144 us -> 1.99 us  [the longest x1 0.74 us: layer(): h2 = jnp.concatenate(ring_gather(h2_own, 'y'), 0)]
    all_gather x2 -> x1, blocking collectives: 68.7 us -> 176 us  [layer(): lax.all_gather(jnp.stack([norm1_gain, norm2_gain], 0), ('z', 'xl', 'y', '...]
  transfers between devices with their start and end apart: 13 -> 122, of which waited for: 8 -> 49; matrix products, arithmetic and copies ran while one was open for 9% -> 22% of each run, Pallas kernels for 0% -> 4%
where the time goes in v1:
time: 795 us; the launch traced here: 784 us
  starting transfers between devices  186 us (23%)
  waiting for transfers between devices  181 us (23%)
  blocking collectives  176 us (22%)
  local copies, waits for them, and re-layouts  80.4 us (10%)
  matrix products  79.9 us (10%)
  other arithmetic  44.7 us (6%)
  Pallas kernels  32.4 us (4%)
    all_gather x1, blocking collectives, layer(): lax.all_gather(jnp.stack([norm1_gain, norm2_gain], 0), ('z', 'xl', 'y', '...  176 us
    ppermute x82, starting transfers between devices, shift(): return lax.ppermute(v, ring, [(i, (i + d) % n) for i in range(n)])  103 us
    ppermute x82, waiting for transfers between devices, shift(): return lax.ppermute(v, ring, [(i, (i + d) % n) for i in range(n)])  86.3 us
    ppermute x32, waiting for transfers between devices, shift(): lax.ppermute(v, X_RING, [(x_index(i), x_index((i + d) % 4)) for i in rang...  73.8 us
    ppermute x32, starting transfers between devices, shift(): lax.ppermute(v, X_RING, [(x_index(i), x_index((i + d) % 4)) for i in rang...  51 us
    dot_general x8, matrix products, dot_tn(): lax.dot_general(a, b, (((0,), (0,)), ((), ())), preferred_element_type=f32)  29 us
    dot_general x8, matrix products, dot(): return jnp.dot(a, b, preferred_element_type=f32)  25.7 us
    dot_general x8, matrix products, dot_nt(): lax.dot_general(a, b, (((1,), (1,)), ((), ())), preferred_element_type=f32)  25.2 us
  transfers between devices with their start and end apart: 122, of which 49 were waited for; matrix products, arithmetic and copies ran while one was open for 22% of the time, Pallas kernels for 4%

profile of v1, /device:TPU:0, one launch (start us, length us, event | category | flops | bytes accessed | tf_op | source)
XLA Modules:
  0.0 784.1 jit_solution(13239915459129980177)
XLA Ops:
  13.6 3.3 all-to-all-start
  21.4 175.5 %all-gather = bf16[64,32,2]{1,2,0:T(2,128)(2,1)S(1)} all-gather(bf16[1,32,2]{1,2,0:T(2,128)(2,1)S(1)} %maximum_bitcast_fusion.11), channel_id=1, replica_groups=mesh['z'=4,'xl'=2,'y'=4,'xh'=2,'c'=2] {'z','xl','y','xh'}, dimensions={0}, use_global_device_ids=true | all-gather | bytes 8320 | tf_op jit(solution)/shard_map/all_gather | solution.py:293
  208.9 4.6 all-to-all-start.2
  214.1 3.2 collective-permute-start.20
  220.5 4.5 all-to-all-start.1
  249.7 3.7 collective-permute-start.47
  270.0 3.3 collective-permute-start.9
  277.5 3.3 collective-permute-start.26
  292.3 3.3 collective-permute-start.3
  301.5 3.8 collective-permute-done.38
  305.4 3.2 collective-permute-start.41
  308.6 3.3 broadcast_in_dim.166
  315.2 9.9 %collective-permute-done.41 = bf16[4,4,32,1408]{3,2,1,0:T(8,128)(2,1)S(1)} collective-permute-done((bf16[4,4,32,1408]{3,2,1,0:T(8,128)(2,1)S(1)}, bf16[4,4,32,1408]{3,2,1,0:T(8,128)(2,1)S(1)}, u32[]{:S(2)}, u32[]{:S(2)}) %collective-permute-start.41) | collective-permute-done | bytes 1441824 | tf_op jit(solution)/shard_map/ppermute | solution.py:24
  333.2 7.7 collective-permute-done.13.kv2_ref
  341.0 3.5 collective-permute-start.43
  344.5 12.4 %attend.1 = (bf16[512,512]{1,0:T(8,128)(2,1)S(1)}, f32[512,8]{1,0:T(8,128)S(1)}) custom-call(bf16[512,512]{1,0:T(8,128)(2,1)S(1)} %pad_maximum_fusion.10.q_ref, bf16[512,256]{1,0:T(8,128)(2,1)S(1)} %pad_maximum_fusion.26.kv_ref, bf16[512,256]{1,0:T(8,128)(2,1)S(1)} %collective-permute-done.13.kv2_ref, s32[512,1]{1,0:T(8,128)S(1)} %copy.435.qpos_ref, ...), custom_call_target="tpu_custom_call" | custom-call | flops 2147483648 | bytes 2097152 | tf_op jit(solution)/shard_map/attend/pallas_call | solution.py:178
  361.2 14.4 %collective-permute-done.42 = bf16[2,4,32,1408]{3,2,1,0:T(8,128)(2,1)S(1)} collective-permute-done((bf16[2,4,32,1408]{3,2,1,0:T(8,128)(2,1)S(1)}, bf16[2,4,32,1408]{3,2,1,0:T(8,128)(2,1)S(1)}, u32[]{:S(2)}, u32[]{:S(2)}) %collective-permute-start.42) | collective-permute-done | bytes 720928 | tf_op jit(solution)/shard_map/ppermute | solution.py:24
  380.4 5.2 collective-permute-done.30
  385.8 3.8 collective-permute-start.31
  394.2 7.3 collective-permute-done.31
  401.5 3.4 collective-permute-done.29
  406.6 3.4 collective-permute-start.33
  412.8 4.7 copy.448
  417.5 3.8 collective-permute-done.32
  423.4 3.3 collective-permute-start.35
  431.9 6.5 fusion.111
  438.5 4.2 multiply_convert_fusion.3
  442.7 6.6 fusion.112
  451.7 6.4 fusion.18
  458.1 6.5 add_convert_fusion.2
  470.0 3.7 add_convert_fusion.3
  485.0 3.7 collective-permute-start.57
  491.1 4.3 collective-permute-done.66
  496.1 6.9 collective-permute-done.57
  504.1 3.4 multiply_reduce_fusion
  507.5 3.4 constant_dynamic-update-slice_fusion.19
  510.9 3.2 collective-permute-start.68
  514.1 5.6 convolution_convert_fusion
  520.6 3.4 convolution_convert_fusion.1
  524.8 3.3 collective-permute-start.70
  530.9 3.8 collective-permute-done.69
  538.3 20.0 %attend_back.1 = (f32[512,512]{1,0:T(8,128)S(1)}, f32[512,256]{1,0:T(8,128)S(1)}, f32[512,256]{1,0:T(8,128)S(1)}) custom-call(bf16[512,512]{1,0:T(8,128)(2,1)S(1)} %pad_maximum_fusion.10.q_ref, bf16[512,512]{1,0:T(8,128)(2,1)S(1)} %pad_maximum_fusion.17.g_ref, f32[512,8]{1,0:T(8,128)S(1)} %get-tuple-element.17.log_ref, ...), custom_call_target="tpu_custom_call" | custom-call | flops 5368709120 | bytes 4194304 | tf_op jit(solution)/shard_map/attend_back/pallas_call | solution.py:233
  561.8 8.8 %collective-permute-done.71 = bf16[512,256]{1,0:T(8,128)(2,1)S(1)} collective-permute-done((bf16[512,256]{1,0:T(8,128)(2,1)S(1)}, bf16[512,256]{1,0:T(8,128)(2,1)S(1)}, u32[]{:S(2)}, u32[]{:S(2)}) %collective-permute-start.71) | collective-permute-done | bytes 262176 | tf_op jit(solution)/shard_map/ppermute | solution.py:26
  577.9 5.4 all-to-all-start.3
  588.7 4.2 all-to-all-done.3
  593.9 3.7 convolution_convert_fusion.2
  603.1 10.4 %collective-permute-done.75 = bf16[128,2048]{1,0:T(8,128)(2,1)S(1)} collective-permute-done((bf16[128,2048]{1,0:T(8,128)(2,1)S(1)}, bf16[128,2048]{1,0:T(8,128)(2,1)S(1)}, u32[]{:S(2)}, u32[]{:S(2)}) %collective-permute-start.75) | collective-permute-done | bytes 524320 | tf_op jit(solution)/shard_map/ppermute | solution.py:26
  624.1 5.2 add_convert_fusion.1
  638.9 3.3 collective-permute-start.95
  644.3 3.4 collective-permute-done.93
  647.7 3.4 collective-permute-start.108
  651.8 3.9 all-to-all-start.5
  673.1 5.3 collective-permute-done.79
  683.6 5.9 add_convert_fusion
  693.3 9.9 %collective-permute-done.97 = bf16[2,4,32,1408]{3,2,1,0:T(8,128)(2,1)S(1)} collective-permute-done((bf16[2,4,32,1408]{3,2,1,0:T(8,128)(2,1)S(1)}, bf16[2,4,32,1408]{3,2,1,0:T(8,128)(2,1)S(1)}, u32[]{:S(2)}, u32[]{:S(2)}) %collective-permute-start.97) | collective-permute-done | bytes 720928 | tf_op jit(solution)/shard_map/ppermute | solution.py:24
  705.9 3.8 collective-permute-start.100
  719.5 16.1 %collective-permute-done.110 = bf16[2,32,704]{2,1,0:T(8,128)(2,1)S(1)} collective-permute-done((bf16[2,32,704]{2,1,0:T(8,128)(2,1)S(1)}, bf16[2,32,704]{2,1,0:T(8,128)(2,1)S(1)}, u32[]{:S(2)}, u32[]{:S(2)}) %collective-permute-start.110) | collective-permute-done | bytes 90144 | tf_op jit(solution)/shard_map/ppermute | solution.py:24
  737.8 3.7 collective-permute-start.113
  746.1 3.3 all-to-all-start.4
  750.2 5.4 all-to-all-done.4
  759.9 4.1 all-to-all-start.7
  765.9 4.4 all-to-all-done.7
  770.3 3.5 all-to-all-start.6
  777.3 3.7 all-to-all-done.6
  (630 shorter events, 267.0 us)
Async XLA Ops:
  2.8 267.2 %collective-permute-start = (bf16[128,2048]{1,0:T(8,128)(2,1)S(1)}, bf16[128,2048]{1,0:T(8,128)(2,1)}, u32[]{:S(2)}, u32[]{:S(2)}) collective-permute-start(bf16[128,2048]{1,0:T(8,128)(2,1)S(1)} %get-tuple-element.37), channel_id=1, source_target_pairs={{0,4},{4,8},{8,12},{12,0},{1,5},{5,9},{9,13},{13,1},{2,6},{6,10},{... | collective-permute-start | bytes 1572872 | tf_op jit(solution)/shard_map/ppermute | solution.py:26
  4.5 269.9 %collective-permute-start.1 = (bf16[128,2048]{1,0:T(8,128)(2,1)S(1)}, bf16[128,2048]{1,0:T(8,128)(2,1)}, u32[]{:S(2)}, u32[]{:S(2)}) collective-permute-start(bf16[128,2048]{1,0:T(8,128)(2,1)S(1)} %get-tuple-element.37), channel_id=1, source_target_pairs={{0,12},{4,0},{8,4},{12,8},{1,13},{5,1},{9,5},{13,9},{2,14},{6,2},{... | collective-permute-start | bytes 1572872 | tf_op jit(solution)/shard_map/ppermute | solution.py:26
  6.1 192.7 %collective-permute-start.14 = (s32[128,1]{0,1:T(1,128)S(1)}, s32[128,1]{0,1:T(1,128)S(1)}, u32[]{:S(2)}, u32[]{:S(2)}) collective-permute-start(s32[128,1]{0,1:T(1,128)S(1)} %fusion.78), channel_id=1, source_target_pairs={{0,4},{4,8},{8,12},{12,0},{1,5},{5,9},{9,13},{13,1},{2,6},{6,10},{... | collective-permute-start | bytes 1544 | tf_op jit(solution)/shard_map/ppermute | solution.py:26
  6.6 192.3 %collective-permute-start.15 = (s32[128,1]{0,1:T(1,128)S(1)}, s32[128,1]{0,1:T(1,128)S(1)}, u32[]{:S(2)}, u32[]{:S(2)}) collective-permute-start(s32[128,1]{0,1:T(1,128)S(1)} %fusion.78), channel_id=1, source_target_pairs={{0,12},{4,0},{8,4},{12,8},{1,13},{5,1},{9,5},{13,9},{2,14},{6,2},{... | collective-permute-start | bytes 1544 | tf_op jit(solution)/shard_map/ppermute | solution.py:26
  13.6 195.3 %all-to-all-start = ((bf16[4,32,640]{2,1,0:T(8,128)(2,1)}), bf16[4,32,640]{2,1,0:T(8,128)(2,1)S(1)}, u32[]{:S(2)}, u32[]{:S(2)}) async-start(bf16[4,32,640]{2,1,0:T(8,128)(2,1)} %copy.407), calls=%async_computation | async-start | bytes 327680 | tf_op jit(solution)/shard_map/all_to_all | solution.py:299
  17.8 259.7 %collective-permute-start.59 = (bf16[128,2048]{1,0:T(8,128)(2,1)S(1)}, bf16[128,2048]{1,0:T(8,128)(2,1)}, u32[]{:S(2)}, u32[]{:S(2)}) collective-permute-start(bf16[128,2048]{1,0:T(8,128)(2,1)S(1)} %get-tuple-element.31), channel_id=1, source_target_pairs={{0,4},{4,8},{8,12},{12,0},{1,5},{5,9},{9,13},{13,1},{2,6},{6,10},{... | collective-permute-start | bytes 1572872 | tf_op jit(solution)/shard_map/ppermute | solution.py:26
  214.1 12.6 %collective-permute-start.20 = (bf16[4,32,256]{2,1,0:T(8,128)(2,1)}, bf16[4,32,256]{2,1,0:T(8,128)(2,1)S(1)}, u32[]{:S(2)}, u32[]{:S(2)}) collective-permute-start(bf16[4,32,256]{2,1,0:T(8,128)(2,1)} %slice.896), channel_id=1, source_target_pairs={{0,18},{16,0},{2,16},{18,2},{1,19},{17,1},{3,17},{19,3},{4,22},{20... | collective-permute-start | bytes 196616 | tf_op jit(solution)/shard_map/ppermute | solution.py:24
  220.5 21.4 %all-to-all-start.1 = ((bf16[4,32,1408]{2,1,0:T(8,128)(2,1)}), bf16[4,32,1408]{2,1,0:T(8,128)(2,1)}, u32[]{:S(2)}, u32[]{:S(2)}) async-start(bf16[4,32,1408]{2,1,0:T(8,128)(2,1)} %copy.440), calls=%async_computation.1 | async-start | bytes 720896 | tf_op jit(solution)/shard_map/all_to_all | solution.py:299
  265.7 16.1 %collective-permute-start.60 = (bf16[128,2048]{1,0:T(8,128)(2,1)S(1)}, bf16[128,2048]{1,0:T(8,128)(2,1)S(1)}, u32[]{:S(2)}, u32[]{:S(2)}) collective-permute-start(bf16[128,2048]{1,0:T(8,128)(2,1)S(1)} %get-tuple-element.31), channel_id=1, source_target_pairs={{0,12},{4,0},{8,4},{12,8},{1,13},{5,1},{9,5},{13,9},{2,14},{6,2},{... | collective-permute-start | bytes 1572872 | tf_op jit(solution)/shard_map/ppermute | solution.py:26
  269.2 26.4 %collective-permute-start.8 = (bf16[4,4,32,384]{3,2,1,0:T(8,128)(2,1)S(1)}, bf16[4,4,32,384]{3,2,1,0:T(8,128)(2,1)S(1)}, u32[]{:S(2)}, u32[]{:S(2)}) collective-permute-start(bf16[4,4,32,384]{3,2,1,0:T(8,128)(2,1)S(1)} %fusion.67), channel_id=1, source_target_pairs={{0,16},{16,2},{2,18},{18,0},{1,17},{17,3},{3,19},{19,1},{4,20},{20... | collective-permute-start | bytes 1179656 | tf_op jit(solution)/shard_map/ppermute | solution.py:24
  270.0 28.5 %collective-permute-start.9 = (bf16[4,4,32,384]{3,2,1,0:T(8,128)(2,1)S(1)}, bf16[4,4,32,384]{3,2,1,0:T(8,128)(2,1)S(1)}, u32[]{:S(2)}, u32[]{:S(2)}) collective-permute-start(bf16[4,4,32,384]{3,2,1,0:T(8,128)(2,1)S(1)} %fusion.67), channel_id=1, source_target_pairs={{0,18},{16,0},{2,16},{18,2},{1,19},{17,1},{3,17},{19,3},{4,22},{20... | collective-permute-start | bytes 1179656 | tf_op jit(solution)/shard_map/ppermute | solution.py:24
  274.4 14.4 %collective-permute-start.36 = (bf16[4,32,1408]{2,1,0:T(8,128)(2,1)}, bf16[4,32,1408]{2,1,0:T(8,128)(2,1)S(1)}, u32[]{:S(2)}, u32[]{:S(2)}) collective-permute-start(bf16[4,32,1408]{2,1,0:T(8,128)(2,1)} %all-to-all-done.1), channel_id=1, source_target_pairs={{0,32},{32,64},{64,96},{96,0},{1,33},{33,65},{65,97},{97,1},{2,34}... | collective-permute-start | bytes 1081352 | tf_op jit(solution)/shard_map/ppermute | solution.py:26
  288.0 104.0 %collective-permute-start.48 = (bf16[2,4,2,32,704]{4,3,2,1,0:T(8,128)(2,1)S(1)}, bf16[2,4,2,32,704]{4,3,2,1,0:T(8,128)(2,1)S(1)}, u32[]{:S(2)}, u32[]{:S(2)}) collective-permute-start(bf16[2,4,2,32,704]{4,3,2,1,0:T(8,128)(2,1)S(1)} %fusion.60), channel_id=1, source_target_pairs={{0,32},{32,64},{64,96},{96,0},{1,33},{33,65},{65,97},{97,1},{2,34}... | collective-permute-start | bytes 2162696 | tf_op jit(solution)/shard_map/ppermute | solution.py:26
  298.7 14.5 %collective-permute-start.11 = (bf16[2,4,32,384]{3,2,1,0:T(8,128)(2,1)S(1)}, bf16[2,4,32,384]{3,2,1,0:T(8,128)(2,1)S(1)}, u32[]{:S(2)}, u32[]{:S(2)}) collective-permute-start(bf16[2,4,32,384]{3,2,1,0:T(8,128)(2,1)S(1)} %slice.875), channel_id=1, source_target_pairs={{0,18},{16,0},{2,16},{18,2},{1,19},{17,1},{3,17},{19,3},{4,22},{20... | collective-permute-start | bytes 589832 | tf_op jit(solution)/shard_map/ppermute | solution.py:24
  299.5 13.7 %collective-permute-start.10 = (bf16[2,4,32,384]{3,2,1,0:T(8,128)(2,1)S(1)}, bf16[2,4,32,384]{3,2,1,0:T(8,128)(2,1)S(1)}, u32[]{:S(2)}, u32[]{:S(2)}) collective-permute-start(bf16[2,4,32,384]{3,2,1,0:T(8,128)(2,1)S(1)} %slice.874), channel_id=1, source_target_pairs={{0,16},{16,2},{2,18},{18,0},{1,17},{17,3},{3,19},{19,1},{4,20},{20... | collective-permute-start | bytes 589832 | tf_op jit(solution)/shard_map/ppermute | solution.py:24
  305.3 20.3 %collective-permute-start.40 = (bf16[4,4,32,1408]{3,2,1,0:T(8,128)(2,1)S(1)}, bf16[4,4,32,1408]{3,2,1,0:T(8,128)(2,1)S(1)}, u32[]{:S(2)}, u32[]{:S(2)}) collective-permute-start(bf16[4,4,32,1408]{3,2,1,0:T(8,128)(2,1)S(1)} %fusion.43), channel_id=1, source_target_pairs={{0,16},{16,2},{2,18},{18,0},{1,17},{17,3},{3,19},{19,1},{4,20},{20... | collective-permute-start | bytes 4325384 | tf_op jit(solution)/shard_map/ppermute | solution.py:24
  305.4 19.8 %collective-permute-start.41 = (bf16[4,4,32,1408]{3,2,1,0:T(8,128)(2,1)S(1)}, bf16[4,4,32,1408]{3,2,1,0:T(8,128)(2,1)S(1)}, u32[]{:S(2)}, u32[]{:S(2)}) collective-permute-start(bf16[4,4,32,1408]{3,2,1,0:T(8,128)(2,1)S(1)} %fusion.43), channel_id=1, source_target_pairs={{0,18},{16,0},{2,16},{18,2},{1,19},{17,1},{3,17},{19,3},{4,22},{20... | collective-permute-start | bytes 4325384 | tf_op jit(solution)/shard_map/ppermute | solution.py:24
  313.2 78.7 %collective-permute-start.49 = (bf16[2,4,2,32,704]{4,3,2,1,0:T(8,128)(2,1)S(1)}, bf16[2,4,2,32,704]{4,3,2,1,0:T(8,128)(2,1)S(1)}, u32[]{:S(2)}, u32[]{:S(2)}) collective-permute-start(bf16[2,4,2,32,704]{4,3,2,1,0:T(8,128)(2,1)S(1)} %fusion.60), channel_id=1, source_target_pairs={{0,96},{32,0},{64,32},{96,64},{1,97},{33,1},{65,33},{97,65},{2,98}... | collective-permute-start | bytes 2162696 | tf_op jit(solution)/shard_map/ppermute | solution.py:26
  313.3 15.3 %collective-permute-start.12 = (bf16[2048,384]{1,0:T(8,128)(2,1)S(1)}, bf16[2048,384]{1,0:T(8,128)(2,1)S(1)}, u32[]{:S(2)}, u32[]{:S(2)}) collective-permute-start(bf16[2048,384]{1,0:T(8,128)(2,1)S(1)} %bitcast.447), channel_id=1, source_target_pairs={{0,1},{1,0},{2,3},{3,2},{4,5},{5,4},{6,7},{7,6},{8,9},{9,8},{10,11... | collective-permute-start | bytes 4718600 | tf_op jit(solution)/shard_map/ppermute | solution.py:26
  325.1 60.7 %collective-permute-start.61 = (bf16[64,2048]{1,0:T(8,128)(2,1)S(1)}, bf16[64,2048]{1,0:T(8,128)(2,1)S(1)}, u32[]{:S(2)}, u32[]{:S(2)}) collective-permute-start(bf16[64,2048]{1,0:T(8,128)(2,1)S(1)} %slice.930), channel_id=1, source_target_pairs={{0,4},{4,8},{8,12},{12,0},{1,5},{5,9},{9,13},{13,1},{2,6},{6,10},{... | collective-permute-start | bytes 786440 | tf_op jit(solution)/shard_map/ppermute | solution.py:26
  325.6 31.2 %collective-permute-start.27 = (bf16[2048,256]{1,0:T(8,128)(2,1)}, bf16[2048,256]{1,0:T(8,128)(2,1)S(1)}, u32[]{:S(2)}, u32[]{:S(2)}) collective-permute-start(bf16[2048,256]{1,0:T(8,128)(2,1)} %bitcast.39), channel_id=1, source_target_pairs={{0,1},{1,0},{2,3},{3,2},{4,5},{5,4},{6,7},{7,6},{8,9},{9,8},{10,11... | collective-permute-start | bytes 3145736 | tf_op jit(solution)/shard_map/ppermute | solution.py:26
  341.0 19.0 %collective-permute-start.43 = (bf16[2,4,32,1408]{3,2,1,0:T(8,128)(2,1)S(1)}, bf16[2,4,32,1408]{3,2,1,0:T(8,128)(2,1)S(1)}, u32[]{:S(2)}, u32[]{:S(2)}) collective-permute-start(bf16[2,4,32,1408]{3,2,1,0:T(8,128)(2,1)S(1)} %slice.914), channel_id=1, source_target_pairs={{0,18},{16,0},{2,16},{18,2},{1,19},{17,1},{3,17},{19,3},{4,22},{20... | collective-permute-start | bytes 2162696 | tf_op jit(solution)/shard_map/ppermute | solution.py:24
  356.9 18.8 %collective-permute-start.42 = (bf16[2,4,32,1408]{3,2,1,0:T(8,128)(2,1)S(1)}, bf16[2,4,32,1408]{3,2,1,0:T(8,128)(2,1)S(1)}, u32[]{:S(2)}, u32[]{:S(2)}) collective-permute-start(bf16[2,4,32,1408]{3,2,1,0:T(8,128)(2,1)S(1)} %slice.913), channel_id=1, source_target_pairs={{0,16},{16,2},{2,18},{18,0},{1,17},{17,3},{3,19},{19,1},{4,20},{20... | collective-permute-start | bytes 2162696 | tf_op jit(solution)/shard_map/ppermute | solution.py:24
  360.0 20.1 %collective-permute-start.28 = (bf16[64,2048]{1,0:T(8,128)(2,1)S(1)}, bf16[64,2048]{1,0:T(8,128)(2,1)S(1)}, u32[]{:S(2)}, u32[]{:S(2)}) collective-permute-start(bf16[64,2048]{1,0:T(8,128)(2,1)S(1)} %get-tuple-element.77), channel_id=1, source_target_pairs={{0,4},{4,8},{8,12},{12,0},{1,5},{5,9},{9,13},{13,1},{2,6},{6,10},{... | collective-permute-start | bytes 786440 | tf_op jit(solution)/shard_map/ppermute | solution.py:26
  385.6 57.1 %collective-permute-start.52 = (bf16[2048,1408]{1,0:T(8,128)(2,1)}, bf16[2048,1408]{1,0:T(8,128)(2,1)}, u32[]{:S(2)}, u32[]{:S(2)}) collective-permute-start(bf16[2048,1408]{1,0:T(8,128)(2,1)} %bitcast.53), channel_id=1, source_target_pairs={{0,1},{1,0},{2,3},{3,2},{4,5},{5,4},{6,7},{7,6},{8,9},{9,8},{10,11... | collective-permute-start | bytes 17301512 | tf_op jit(solution)/shard_map/ppermute | solution.py:26
  385.8 15.6 %collective-permute-start.31 = (bf16[128,2048]{1,0:T(8,128)(2,1)S(1)}, bf16[128,2048]{1,0:T(8,128)(2,1)S(1)}, u32[]{:S(2)}, u32[]{:S(2)}) collective-permute-start(bf16[128,2048]{1,0:T(8,128)(2,1)S(1)} %pad_maximum_fusion.12), channel_id=1, source_target_pairs={{0,12},{4,0},{8,4},{12,8},{1,13},{5,1},{9,5},{13,9},{2,14},{6,2},{... | collective-permute-start | bytes 1572872 | tf_op jit(solution)/shard_map/ppermute | solution.py:26
  389.6 15.3 %collective-permute-start.29 = (bf16[128,2048]{1,0:T(8,128)(2,1)S(1)}, bf16[128,2048]{1,0:T(8,128)(2,1)S(1)}, u32[]{:S(2)}, u32[]{:S(2)}) collective-permute-start(bf16[128,2048]{1,0:T(8,128)(2,1)S(1)} %pad_maximum_fusion.11), channel_id=1, source_target_pairs={{0,4},{4,8},{8,12},{12,0},{1,5},{5,9},{9,13},{13,1},{2,6},{6,10},{... | collective-permute-start | bytes 1572872 | tf_op jit(solution)/shard_map/ppermute | solution.py:26
  392.0 19.9 %collective-permute-start.51 = (bf16[1,4,2,32,704]{4,3,2,1,0:T(8,128)(2,1)S(1)}, bf16[1,4,2,32,704]{4,3,2,1,0:T(8,128)(2,1)S(1)}, u32[]{:S(2)}, u32[]{:S(2)}) collective-permute-start(bf16[1,4,2,32,704]{4,3,2,1,0:T(8,128)(2,1)S(1)} %slice.920), channel_id=1, source_target_pairs={{0,96},{32,0},{64,32},{96,64},{1,97},{33,1},{65,33},{97,65},{2,98}... | collective-permute-start | bytes 1081352 | tf_op jit(solution)/shard_map/ppermute | solution.py:26
  392.1 19.8 %collective-permute-start.50 = (bf16[1,4,2,32,704]{4,3,2,1,0:T(8,128)(2,1)S(1)}, bf16[1,4,2,32,704]{4,3,2,1,0:T(8,128)(2,1)S(1)}, u32[]{:S(2)}, u32[]{:S(2)}) collective-permute-start(bf16[1,4,2,32,704]{4,3,2,1,0:T(8,128)(2,1)S(1)} %slice.919), channel_id=1, source_target_pairs={{0,32},{32,64},{64,96},{96,0},{1,33},{33,65},{65,97},{97,1},{2,34}... | collective-permute-start | bytes 1081352 | tf_op jit(solution)/shard_map/ppermute | solution.py:26
  406.6 14.8 %collective-permute-start.32 = (bf16[128,2048]{1,0:T(8,128)(2,1)}, bf16[128,2048]{1,0:T(8,128)(2,1)}, u32[]{:S(2)}, u32[]{:S(2)}) collective-permute-start(bf16[128,2048]{1,0:T(8,128)(2,1)} %get-tuple-element.33), channel_id=1, source_target_pairs={{0,4},{4,8},{8,12},{12,0},{1,5},{5,9},{9,13},{13,1},{2,6},{6,10},{... | collective-permute-start | bytes 1572872 | tf_op jit(solution)/shard_map/ppermute | solution.py:26
  406.6 15.8 %collective-permute-start.33 = (bf16[128,2048]{1,0:T(8,128)(2,1)}, bf16[128,2048]{1,0:T(8,128)(2,1)}, u32[]{:S(2)}, u32[]{:S(2)}) collective-permute-start(bf16[128,2048]{1,0:T(8,128)(2,1)} %get-tuple-element.33), channel_id=1, source_target_pairs={{0,12},{4,0},{8,4},{12,8},{1,13},{5,1},{9,5},{13,9},{2,14},{6,2},{... | collective-permute-start | bytes 1572872 | tf_op jit(solution)/shard_map/ppermute | solution.py:26
  417.5 31.9 %collective-permute-start.53 = (bf16[2048,704]{0,1:T(8,128)(2,1)}, bf16[2048,704]{0,1:T(8,128)(2,1)S(1)}, u32[]{:S(2)}, u32[]{:S(2)}) collective-permute-start(bf16[2048,704]{0,1:T(8,128)(2,1)} %copy.448), channel_id=1, source_target_pairs={{0,1},{1,0},{2,3},{3,2},{4,5},{5,4},{6,7},{7,6},{8,9},{9,8},{10,11... | collective-permute-start | bytes 8650760 | tf_op jit(solution)/shard_map/ppermute | solution.py:26
  464.7 12.5 %collective-permute-start.63 = (bf16[64,2048]{1,0:T(8,128)(2,1)S(1)}, bf16[64,2048]{1,0:T(8,128)(2,1)S(1)}, u32[]{:S(2)}, u32[]{:S(2)}) collective-permute-start(bf16[64,2048]{1,0:T(8,128)(2,1)S(1)} %get-tuple-element.65), channel_id=1, source_target_pairs={{0,4},{4,8},{8,12},{12,0},{1,5},{5,9},{9,13},{13,1},{2,6},{6,10},{... | collective-permute-start | bytes 786440 | tf_op jit(solution)/shard_map/ppermute | solution.py:26
  478.2 17.1 %collective-permute-start.66 = (bf16[128,2048]{1,0:T(8,128)(2,1)}, bf16[128,2048]{1,0:T(8,128)(2,1)}, u32[]{:S(2)}, u32[]{:S(2)}) collective-permute-start(bf16[128,2048]{1,0:T(8,128)(2,1)} %pad_maximum_fusion.16), channel_id=1, source_target_pairs={{0,12},{4,0},{8,4},{12,8},{1,13},{5,1},{9,5},{13,9},{2,14},{6,2},{... | collective-permute-start | bytes 1572872 | tf_op jit(solution)/shard_map/ppermute | solution.py:26
  479.7 16.4 %collective-permute-start.64 = (bf16[128,2048]{1,0:T(8,128)(2,1)}, bf16[128,2048]{1,0:T(8,128)(2,1)}, u32[]{:S(2)}, u32[]{:S(2)}) collective-permute-start(bf16[128,2048]{1,0:T(8,128)(2,1)} %pad_maximum_fusion.15), channel_id=1, source_target_pairs={{0,4},{4,8},{8,12},{12,0},{1,5},{5,9},{9,13},{13,1},{2,6},{6,10},{... | collective-permute-start | bytes 1572872 | tf_op jit(solution)/shard_map/ppermute | solution.py:26
  485.0 18.0 %collective-permute-start.57 = (bf16[128,2048]{1,0:T(8,128)(2,1)}, bf16[128,2048]{1,0:T(8,128)(2,1)}, u32[]{:S(2)}, u32[]{:S(2)}) collective-permute-start(bf16[128,2048]{1,0:T(8,128)(2,1)} %pad_maximum_fusion.14), channel_id=1, source_target_pairs={{0,12},{4,0},{8,4},{12,8},{1,13},{5,1},{9,5},{13,9},{2,14},{6,2},{... | collective-permute-start | bytes 1572872 | tf_op jit(solution)/shard_map/ppermute | solution.py:26
  489.5 14.6 %collective-permute-start.55 = (bf16[128,2048]{1,0:T(8,128)(2,1)}, bf16[128,2048]{1,0:T(8,128)(2,1)}, u32[]{:S(2)}, u32[]{:S(2)}) collective-permute-start(bf16[128,2048]{1,0:T(8,128)(2,1)} %pad_maximum_fusion.13), channel_id=1, source_target_pairs={{0,4},{4,8},{8,12},{12,0},{1,5},{5,9},{9,13},{13,1},{2,6},{6,10},{... | collective-permute-start | bytes 1572872 | tf_op jit(solution)/shard_map/ppermute | solution.py:26
  510.9 13.8 %collective-permute-start.67 = (bf16[128,2048]{1,0:T(8,128)(2,1)}, bf16[128,2048]{1,0:T(8,128)(2,1)S(1)}, u32[]{:S(2)}, u32[]{:S(2)}) collective-permute-start(bf16[128,2048]{1,0:T(8,128)(2,1)} %get-tuple-element.28), channel_id=1, source_target_pairs={{0,4},{4,8},{8,12},{12,0},{1,5},{5,9},{9,13},{13,1},{2,6},{6,10},{... | collective-permute-start | bytes 1572872 | tf_op jit(solution)/shard_map/ppermute | solution.py:26
  510.9 13.9 %collective-permute-start.68 = (bf16[128,2048]{1,0:T(8,128)(2,1)}, bf16[128,2048]{1,0:T(8,128)(2,1)S(1)}, u32[]{:S(2)}, u32[]{:S(2)}) collective-permute-start(bf16[128,2048]{1,0:T(8,128)(2,1)} %get-tuple-element.28), channel_id=1, source_target_pairs={{0,12},{4,0},{8,4},{12,8},{1,13},{5,1},{9,5},{13,9},{2,14},{6,2},{... | collective-permute-start | bytes 1572872 | tf_op jit(solution)/shard_map/ppermute | solution.py:26
  514.1 14.0 %collective-permute-start.58 = (bf16[128,2048]{1,0:T(8,128)(2,1)}, bf16[128,2048]{1,0:T(8,128)(2,1)}, u32[]{:S(2)}, u32[]{:S(2)}) collective-permute-start(bf16[128,2048]{1,0:T(8,128)(2,1)} %get-tuple-element.104), channel_id=1, source_target_pairs={{0,1},{1,0},{2,3},{3,2},{4,5},{5,4},{6,7},{7,6},{8,9},{9,8},{10,11... | collective-permute-start | bytes 1572872 | tf_op jit(solution)/shard_map/ppermute | solution.py:26
  519.7 162.5 %collective-permute-start.96 = (bf16[2048,1408]{1,0:T(8,128)(2,1)}, bf16[2048,1408]{1,0:T(8,128)(2,1)}, u32[]{:S(2)}, u32[]{:S(2)}) collective-permute-start(bf16[2048,1408]{1,0:T(8,128)(2,1)} %convolution_convert_fusion), channel_id=1, source_target_pairs={{0,1},{1,0},{2,3},{3,2},{4,5},{5,4},{6,7},{7,6},{8,9},{9,8},{10,11... | collective-permute-start | bytes 17301512 | tf_op jit(solution)/shard_map/ppermute | solution.py:26
  524.0 99.9 %collective-permute-start.105 = (bf16[2048,704]{0,1:T(8,128)(2,1)}, bf16[2048,704]{0,1:T(8,128)(2,1)}, u32[]{:S(2)}, u32[]{:S(2)}) collective-permute-start(bf16[2048,704]{0,1:T(8,128)(2,1)} %convolution_convert_fusion.1), channel_id=1, source_target_pairs={{0,1},{1,0},{2,3},{3,2},{4,5},{5,4},{6,7},{7,6},{8,9},{9,8},{10,11... | collective-permute-start | bytes 8650760 | tf_op jit(solution)/shard_map/ppermute | solution.py:26
  577.9 15.0 %all-to-all-start.3 = ((f32[64,2,32]{2,1,0:T(2,128)}), f32[64,2,32]{2,1,0:T(2,128)}, u32[]{:S(2)}, u32[]{:S(2)}) async-start(f32[64,2,32]{2,1,0:T(2,128)} %copy.463), calls=%async_computation.3 | async-start | bytes 131072 | tf_op jit(solution)/shard_map/all_to_all | solution.py:403
  585.4 12.6 %collective-permute-start.72 = (bf16[64,2048]{1,0:T(8,128)(2,1)}, bf16[64,2048]{1,0:T(8,128)(2,1)}, u32[]{:S(2)}, u32[]{:S(2)}) collective-permute-start(bf16[64,2048]{1,0:T(8,128)(2,1)} %get-tuple-element.59), channel_id=1, source_target_pairs={{0,4},{4,8},{8,12},{12,0},{1,5},{5,9},{9,13},{13,1},{2,6},{6,10},{... | collective-permute-start | bytes 786440 | tf_op jit(solution)/shard_map/ppermute | solution.py:26
  599.4 14.0 %collective-permute-start.75 = (bf16[128,2048]{1,0:T(8,128)(2,1)S(1)}, bf16[128,2048]{1,0:T(8,128)(2,1)S(1)}, u32[]{:S(2)}, u32[]{:S(2)}) collective-permute-start(bf16[128,2048]{1,0:T(8,128)(2,1)S(1)} %pad_maximum_fusion.19), channel_id=1, source_target_pairs={{0,12},{4,0},{8,4},{12,8},{1,13},{5,1},{9,5},{13,9},{2,14},{6,2},{... | collective-permute-start | bytes 1572872 | tf_op jit(solution)/shard_map/ppermute | solution.py:26
  600.7 15.0 %collective-permute-start.73 = (bf16[128,2048]{1,0:T(8,128)(2,1)S(1)}, bf16[128,2048]{1,0:T(8,128)(2,1)S(1)}, u32[]{:S(2)}, u32[]{:S(2)}) collective-permute-start(bf16[128,2048]{1,0:T(8,128)(2,1)S(1)} %pad_maximum_fusion.18), channel_id=1, source_target_pairs={{0,4},{4,8},{8,12},{12,0},{1,5},{5,9},{9,13},{13,1},{2,6},{6,10},{... | collective-permute-start | bytes 1572872 | tf_op jit(solution)/shard_map/ppermute | solution.py:26
  602.2 64.5 %collective-permute-start.78 = (bf16[2048,384]{1,0:T(8,128)(2,1)}, bf16[2048,384]{1,0:T(8,128)(2,1)}, u32[]{:S(2)}, u32[]{:S(2)}) collective-permute-start(bf16[2048,384]{1,0:T(8,128)(2,1)} %convolution_convert_fusion.2), channel_id=1, source_target_pairs={{0,1},{1,0},{2,3},{3,2},{4,5},{5,4},{6,7},{7,6},{8,9},{9,8},{10,11... | collective-permute-start | bytes 4718600 | tf_op jit(solution)/shard_map/ppermute | solution.py:26
  619.6 36.1 %collective-permute-start.76 = (bf16[128,2048]{1,0:T(8,128)(2,1)}, bf16[128,2048]{1,0:T(8,128)(2,1)}, u32[]{:S(2)}, u32[]{:S(2)}) collective-permute-start(bf16[128,2048]{1,0:T(8,128)(2,1)} %fusion.16), channel_id=1, source_target_pairs={{0,1},{1,0},{2,3},{3,2},{4,5},{5,4},{6,7},{7,6},{8,9},{9,8},{10,11... | collective-permute-start | bytes 1572872 | tf_op jit(solution)/shard_map/ppermute | solution.py:26
  644.1 18.9 %collective-permute-start.106 = (bf16[1,4,2,32,704]{4,3,2,1,0:T(8,128)(2,1)}, bf16[1,4,2,32,704]{4,3,2,1,0:T(8,128)(2,1)}, u32[]{:S(2)}, u32[]{:S(2)}) collective-permute-start(bf16[1,4,2,32,704]{4,3,2,1,0:T(8,128)(2,1)} %get-tuple-element.51), channel_id=1, source_target_pairs={{0,32},{32,64},{64,96},{96,0},{1,33},{33,65},{65,97},{97,1},{2,34}... | collective-permute-start | bytes 1081352 | tf_op jit(solution)/shard_map/ppermute | solution.py:26
  647.7 15.2 %collective-permute-start.108 = (bf16[1,4,2,32,704]{4,3,2,1,0:T(8,128)(2,1)}, bf16[1,4,2,32,704]{4,3,2,1,0:T(8,128)(2,1)}, u32[]{:S(2)}, u32[]{:S(2)}) collective-permute-start(bf16[1,4,2,32,704]{4,3,2,1,0:T(8,128)(2,1)} %get-tuple-element.53), channel_id=1, source_target_pairs={{0,96},{32,0},{64,32},{96,64},{1,97},{33,1},{65,33},{97,65},{2,98}... | collective-permute-start | bytes 1081352 | tf_op jit(solution)/shard_map/ppermute | solution.py:26
  664.5 17.3 %collective-permute-start.109 = (bf16[2,4,2,32,704]{4,3,2,1,0:T(8,128)(2,1)S(1)}, bf16[2,4,2,32,704]{4,3,2,1,0:T(8,128)(2,1)S(1)}, u32[]{:S(2)}, u32[]{:S(2)}) collective-permute-start(bf16[2,4,2,32,704]{4,3,2,1,0:T(8,128)(2,1)S(1)} %pad_maximum_fusion.9), channel_id=1, source_target_pairs={{0,96},{32,0},{64,32},{96,64},{1,97},{33,1},{65,33},{97,65},{2,98}... | collective-permute-start | bytes 2162696 | tf_op jit(solution)/shard_map/ppermute | solution.py:26
  664.6 17.1 %collective-permute-start.107 = (bf16[2,4,2,32,704]{4,3,2,1,0:T(8,128)(2,1)S(1)}, bf16[2,4,2,32,704]{4,3,2,1,0:T(8,128)(2,1)S(1)}, u32[]{:S(2)}, u32[]{:S(2)}) collective-permute-start(bf16[2,4,2,32,704]{4,3,2,1,0:T(8,128)(2,1)S(1)} %pad_maximum_fusion.8), channel_id=1, source_target_pairs={{0,32},{32,64},{64,96},{96,0},{1,33},{33,65},{65,97},{97,1},{2,34}... | collective-permute-start | bytes 2162696 | tf_op jit(solution)/shard_map/ppermute | solution.py:26
  678.6 31.5 %collective-permute-start.82 = (bf16[4,4,32,384]{3,2,1,0:T(8,128)(2,1)S(1)}, bf16[4,4,32,384]{3,2,1,0:T(8,128)(2,1)S(1)}, u32[]{:S(2)}, u32[]{:S(2)}) collective-permute-start(bf16[4,4,32,384]{3,2,1,0:T(8,128)(2,1)S(1)} %pad_maximum_fusion.23), channel_id=1, source_target_pairs={{0,18},{16,0},{2,16},{18,2},{1,19},{17,1},{3,17},{19,3},{4,22},{20... | collective-permute-start | bytes 1179656 | tf_op jit(solution)/shard_map/ppermute | solution.py:24
  681.4 28.7 %collective-permute-start.80 = (bf16[4,4,32,384]{3,2,1,0:T(8,128)(2,1)S(1)}, bf16[4,4,32,384]{3,2,1,0:T(8,128)(2,1)S(1)}, u32[]{:S(2)}, u32[]{:S(2)}) collective-permute-start(bf16[4,4,32,384]{3,2,1,0:T(8,128)(2,1)S(1)} %pad_maximum_fusion.22), channel_id=1, source_target_pairs={{0,16},{16,2},{2,18},{18,0},{1,17},{17,3},{3,19},{19,1},{4,20},{20... | collective-permute-start | bytes 1179656 | tf_op jit(solution)/shard_map/ppermute | solution.py:24
  689.8 13.4 %collective-permute-start.97 = (bf16[2,4,32,1408]{3,2,1,0:T(8,128)(2,1)S(1)}, bf16[2,4,32,1408]{3,2,1,0:T(8,128)(2,1)S(1)}, u32[]{:S(2)}, u32[]{:S(2)}) collective-permute-start(bf16[2,4,32,1408]{3,2,1,0:T(8,128)(2,1)S(1)} %get-tuple-element.40), channel_id=1, source_target_pairs={{0,16},{16,2},{2,18},{18,0},{1,17},{17,3},{3,19},{19,1},{4,20},{20... | collective-permute-start | bytes 2162696 | tf_op jit(solution)/shard_map/ppermute | solution.py:24
  689.9 15.5 %collective-permute-start.99 = (bf16[2,4,32,1408]{3,2,1,0:T(8,128)(2,1)S(1)}, bf16[2,4,32,1408]{3,2,1,0:T(8,128)(2,1)S(1)}, u32[]{:S(2)}, u32[]{:S(2)}) collective-permute-start(bf16[2,4,32,1408]{3,2,1,0:T(8,128)(2,1)S(1)} %get-tuple-element.42), channel_id=1, source_target_pairs={{0,18},{16,0},{2,16},{18,2},{1,19},{17,1},{3,17},{19,3},{4,22},{20... | collective-permute-start | bytes 2162696 | tf_op jit(solution)/shard_map/ppermute | solution.py:24
  705.9 35.6 %collective-permute-start.100 = (bf16[4,4,32,1408]{3,2,1,0:T(8,128)(2,1)S(1)}, bf16[4,4,32,1408]{3,2,1,0:T(8,128)(2,1)S(1)}, u32[]{:S(2)}, u32[]{:S(2)}) collective-permute-start(bf16[4,4,32,1408]{3,2,1,0:T(8,128)(2,1)S(1)} %pad_maximum_fusion.3), channel_id=1, source_target_pairs={{0,18},{16,0},{2,16},{18,2},{1,19},{17,1},{3,17},{19,3},{4,22},{20... | collective-permute-start | bytes 4325384 | tf_op jit(solution)/shard_map/ppermute | solution.py:24
  709.8 31.7 %collective-permute-start.98 = (bf16[4,4,32,1408]{3,2,1,0:T(8,128)(2,1)S(1)}, bf16[4,4,32,1408]{3,2,1,0:T(8,128)(2,1)S(1)}, u32[]{:S(2)}, u32[]{:S(2)}) collective-permute-start(bf16[4,4,32,1408]{3,2,1,0:T(8,128)(2,1)S(1)} %pad_maximum_fusion.2), channel_id=1, source_target_pairs={{0,16},{16,2},{2,18},{18,0},{1,17},{17,3},{3,19},{19,1},{4,20},{20... | collective-permute-start | bytes 4325384 | tf_op jit(solution)/shard_map/ppermute | solution.py:24
  709.9 25.8 %collective-permute-start.110 = (bf16[2,32,704]{2,1,0:T(8,128)(2,1)S(1)}, bf16[2,32,704]{2,1,0:T(8,128)(2,1)S(1)}, u32[]{:S(2)}, u32[]{:S(2)}) collective-permute-start(bf16[2,32,704]{2,1,0:T(8,128)(2,1)S(1)} %get-tuple-element.109), channel_id=1, source_target_pairs={{0,16},{16,2},{2,18},{18,0},{1,17},{17,3},{3,19},{19,1},{4,20},{20... | collective-permute-start | bytes 270344 | tf_op jit(solution)/shard_map/ppermute | solution.py:24
  715.7 21.3 %collective-permute-start.112 = (bf16[2,32,704]{2,1,0:T(8,128)(2,1)S(1)}, bf16[2,32,704]{2,1,0:T(8,128)(2,1)S(1)}, u32[]{:S(2)}, u32[]{:S(2)}) collective-permute-start(bf16[2,32,704]{2,1,0:T(8,128)(2,1)S(1)} %get-tuple-element.111), channel_id=1, source_target_pairs={{0,18},{16,0},{2,16},{18,2},{1,19},{17,1},{3,17},{19,3},{4,22},{20... | collective-permute-start | bytes 270344 | tf_op jit(solution)/shard_map/ppermute | solution.py:24
  718.9 26.6 %collective-permute-start.86 = (bf16[4,32,384]{2,1,0:T(8,128)(2,1)S(1)}, bf16[4,32,384]{2,1,0:T(8,128)(2,1)S(1)}, u32[]{:S(2)}, u32[]{:S(2)}) collective-permute-start(bf16[4,32,384]{2,1,0:T(8,128)(2,1)S(1)} %pad_maximum_fusion.34), channel_id=1, source_target_pairs={{0,96},{32,0},{64,32},{96,64},{1,97},{33,1},{65,33},{97,65},{2,98}... | collective-permute-start | bytes 294920 | tf_op jit(solution)/shard_map/ppermute | solution.py:26
  737.8 20.2 %collective-permute-start.113 = (bf16[4,32,704]{2,1,0:T(8,128)(2,1)}, bf16[4,32,704]{2,1,0:T(8,128)(2,1)}, u32[]{:S(2)}, u32[]{:S(2)}) collective-permute-start(bf16[4,32,704]{2,1,0:T(8,128)(2,1)} %pad_maximum_fusion.30), channel_id=1, source_target_pairs={{0,18},{16,0},{2,16},{18,2},{1,19},{17,1},{3,17},{19,3},{4,22},{20... | collective-permute-start | bytes 540680 | tf_op jit(solution)/shard_map/ppermute | solution.py:24
  742.1 13.4 %collective-permute-start.101 = (bf16[2,32,1408]{2,1,0:T(8,128)(2,1)S(1)}, bf16[2,32,1408]{2,1,0:T(8,128)(2,1)S(1)}, u32[]{:S(2)}, u32[]{:S(2)}) collective-permute-start(bf16[2,32,1408]{2,1,0:T(8,128)(2,1)S(1)} %get-tuple-element.92), channel_id=1, source_target_pairs={{0,32},{32,64},{64,96},{96,0},{1,33},{33,65},{65,97},{97,1},{2,34}... | collective-permute-start | bytes 540680 | tf_op jit(solution)/shard_map/ppermute | solution.py:26
  742.5 13.1 %collective-permute-start.103 = (bf16[2,32,1408]{2,1,0:T(8,128)(2,1)S(1)}, bf16[2,32,1408]{2,1,0:T(8,128)(2,1)S(1)}, u32[]{:S(2)}, u32[]{:S(2)}) collective-permute-start(bf16[2,32,1408]{2,1,0:T(8,128)(2,1)S(1)} %get-tuple-element.94), channel_id=1, source_target_pairs={{0,96},{32,0},{64,32},{96,64},{1,97},{33,1},{65,33},{97,65},{2,98}... | collective-permute-start | bytes 540680 | tf_op jit(solution)/shard_map/ppermute | solution.py:26
  (138 other events, 2310.1 us)
